TPU v7x, 32 devices: a whole 2x2x4 slice. The times are simulated.
32 devices in a mesh: section: 2 (over core), dp: 4 (over z), expert: 4 (over y, x).
Axes of the slice: x: 2, y: 2, z: 4, core: 2. Of those that a mesh axis runs over, the one named last changes fastest.
Arguments:
- ends: bfloat16 [2, 8192, 768], P('section', ('dp', 'expert')), may hold values from -6 to 6
- w_query: bfloat16 [2, 768, 768], P('section', 'dp'), may hold values from -0.21875 to 0.21875
- w_key: bfloat16 [2, 768, 768], P('section', 'dp'), may hold values from -0.21875 to 0.21875
- w_value: bfloat16 [2, 768, 768], P('section', 'dp'), may hold values from -0.21875 to 0.21875
- w_output: bfloat16 [2, 768, 768], P('section', 'dp'), may hold values from -1.25 to 1.25
- gain_attention: bfloat16 [2, 768], P('section', 'dp'), may hold values from 0.5 to 1.5
- gain_experts: bfloat16 [2, 768], P('section', 'dp'), may hold values from 0.5 to 1.5
- router: bfloat16 [2, 768, 4], P('section', 'dp'), may hold values from -0.15625 to 0.15625
- bias_table: bfloat16 [2, 32, 12], P('section', 'dp'), may hold values from -5 to 5
- experts_up: bfloat16 [2, 4, 768, 3072], P('section', 'expert', 'dp'), may hold values from -0.21875 to 0.21875
- experts_down: bfloat16 [2, 4, 3072, 768], P('section', 'expert', None, 'dp'), may hold values from -0.4375 to 0.4375
- routes: int32 [2, 8192], P('section', ('dp', 'expert')), may hold values from 0 to 3, as said below
- slots: int32 [2, 8192], P('section', ('dp', 'expert')), may hold values from 0 to 127, as said below
- segments: int32 [8192], P(('dp', 'expert')), may hold values from 0 to 8191, as said below
- buckets: int32 [511], replicated, may hold values from 0 to 31
Outputs:
- ends_out: bfloat16 [2, 8192, 768], P('section', ('dp', 'expert'))
- grad_w_query: float32 [2, 768, 768], P('section', 'dp')
- grad_w_key: float32 [2, 768, 768], P('section', 'dp')
- grad_w_value: float32 [2, 768, 768], P('section', 'dp')
- grad_w_output: float32 [2, 768, 768], P('section', 'dp')
- grad_gain_attention: float32 [2, 768], P('section', 'dp')
- grad_gain_experts: float32 [2, 768], P('section', 'dp')
- grad_router: float32 [2, 768, 4], P('section', 'dp')
- grad_bias_table: float32 [2, 32, 12], P('section', 'dp')
- grad_experts_up: float32 [2, 4, 768, 3072], P('section', 'expert', 'dp')
- grad_experts_down: float32 [2, 4, 3072, 768], P('section', 'expert', None, 'dp')
Inputs may be any that keep to these rules, and one draw needn't show every extreme that they name: `routes`: blocks are the aligned runs of 256 tokens of one layer (one sequence each), ordered by layer, then device of dp+expert, then micro-batch. In a block, no expert is named by more than 128 tokens. For each layer, micro-batch and index of dp, one expert is named by exactly 128 tokens in every block of the 4 devices of that index. `slots`: within a block, no two tokens have the same route and slot. `segments`: A token's number is the index among all 8192 tokens of the last token of its document; never falling along each sequence of 256 tokens; a document never crosses a sequence's end.
All inputs are finite; a program needn't handle non-finite values.
Results may differ from a plain program's by a relative error of at most 0.028.
Values may be sent and summed in bfloat16 or wider, within the bound.
A program may use at most 192 MiB of HBM per device.

v0:
```python
import jax
import jax.numpy as jnp
from jax import lax
from jax.sharding import PartitionSpec as P

epsilon = 1e-06
highest = lax.Precision.HIGHEST


def from_behind(value, axis, steps):
    count = lax.axis_size(axis)
    first, last = (max(0, -steps), min(count, count - steps))
    return lax.ppermute(value, axis, [(source, source + steps) for source in range(first, last)])


def normalize(values, gain):
    return values * lax.rsqrt(jnp.mean(values * values, axis=-1, keepdims=True) + epsilon) * gain


def gelu_both(values):
    below = 0.5 * (1.0 + lax.erf(values * (0.5**0.5)))
    density = jnp.exp(-0.5 * values * values) * ((2.0 * jnp.pi) ** -0.5)
    return (values * below).astype(jnp.bfloat16), (below + values * density).astype(jnp.bfloat16)


def spread_offsets(table_rows, length):
    heads = table_rows.shape[0]
    widened = jnp.broadcast_to(table_rows[:, None, :], (heads, length, 2 * length - 1)).reshape(
        heads, length * (2 * length - 1)
    )
    widened = jnp.concatenate([widened, jnp.zeros((heads, length), table_rows.dtype)], 1).reshape(
        heads, length, 2 * length
    )
    return widened[:, :, :length][:, :, ::-1]


def offset_sums(grads, length):
    heads = grads.shape[0]
    flipped = grads[:, :, ::-1]
    padded = jnp.concatenate([flipped, jnp.zeros((heads, length, length), grads.dtype)], 2).reshape(
        heads, 2 * length * length
    )
    return padded[:, : length * (2 * length - 1)].reshape(heads, length, 2 * length - 1).sum(1)


def shards(
    ends,
    w_query,
    w_key,
    w_value,
    w_output,
    gain_attention,
    gain_experts,
    router,
    bias_table,
    experts_up,
    experts_down,
    routes,
    slots,
    segments,
    buckets,
):
    section = lax.axis_index("section")
    first = section == 0
    length = (buckets.shape[0] + 1) // 2
    model = ends.shape[2]
    batches = ends.shape[1] // length
    owners = lax.axis_size("expert")
    layers = lax.axis_size("dp")
    mine = lax.axis_index("expert")
    projections = jnp.concatenate([w_query[0], w_key[0], w_value[0], w_output[0]], 1)
    piece = projections.shape[0] // owners
    small = jnp.concatenate(
        [
            gain_attention.reshape(1, -1),
            gain_experts.reshape(1, -1),
            router.reshape(1, -1),
            bias_table.reshape(1, -1),
        ],
        1,
    )
    gathered = lax.all_gather(
        lax.dynamic_slice_in_dim(projections, mine * piece, piece, 0),
        ("dp", "expert"),
        axis=0,
        tiled=True,
    )
    qkv_w = gathered[:, : 3 * model]
    output_w = gathered[:, 3 * model :]
    small = lax.all_gather(small, "dp", axis=0, tiled=True)
    rows = w_query.shape[1]
    kinds = router.shape[2]
    gain_one = small[:, :rows].reshape(-1).astype(jnp.float32)
    gain_two = small[:, rows : 2 * rows].reshape(-1).astype(jnp.float32)
    router_w = small[:, 2 * rows : (2 + kinds) * rows].reshape(-1, kinds)
    table = small[:, (2 + kinds) * rows :].reshape(-1, bias_table.shape[2]).astype(jnp.float32)
    up_w = lax.all_gather(experts_up, "dp", axis=2, tiled=True)[0]
    down_w = lax.all_gather(
        jnp.swapaxes(experts_down[0], 1, 2), "dp", axis=1, tiled=True
    )
    local = up_w.shape[0]
    experts = owners * local
    capacity = 2 * length // experts
    heads = table.shape[1]
    width = model // heads
    scale = width ** (-0.5)
    bucket_hot = (buckets[None, :] == jnp.arange(table.shape[0], dtype=jnp.int32)[:, None]).astype(
        jnp.float32
    )
    relative = spread_offsets(jnp.dot(table.T, bucket_hot, precision=highest), length)
    my_routes = routes[0].reshape(batches, length)
    my_slots = slots[0].reshape(batches, length)
    my_segments = segments.reshape(batches, length)
    data = ends[0].reshape(batches, length, model)
    expert_ids = jnp.arange(experts, dtype=jnp.int32)

    def attention_scores(queries, keys, segment):
        same = segment[:, None] == segment[None, :]
        scores = (
            jnp.einsum("qhd,khd->hqk", queries, keys, preferred_element_type=jnp.float32) * scale
            + relative
        )
        return jnp.where(same[None], scores, -1e30)

    def merged(all_steps):
        ends_step = jax.tree.map(pick, all_steps[batches], all_steps[0])
        return all_steps[1:batches] + [ends_step]

    def product_sum(parts, left, right, form):
        return sum(
            jnp.einsum(form, part[left], part[right], preferred_element_type=jnp.float32)
            for part in parts
        ).astype(jnp.bfloat16)

    def expert_sums(all_steps):
        names = ("arrived", "activated", "arrived_grad", "before_grad")
        parts = merged([{name: each[name] for name in names} for each in all_steps])
        return (
            product_sum(parts, "arrived", "before_grad", "secd,secf->edf"),
            product_sum(parts, "arrived_grad", "activated", "secd,secf->edf"),
        )

    received = jnp.zeros((length, model), jnp.bfloat16)
    stash = []
    produced = []
    for tick in range(batches + 1):
        early = min(tick, batches - 1)
        late = max(tick - 1, 0)
        inputs = jnp.where(first, data[early], received)
        route = jnp.where(first, my_routes[early], my_routes[late])
        slot = jnp.where(first, my_slots[early], my_slots[late])
        segment = jnp.where(first, my_segments[early], my_segments[late])
        current = inputs.astype(jnp.float32)
        forward_normed = normalize(current, gain_one).astype(jnp.bfloat16)
        projected = jnp.dot(forward_normed, qkv_w, preferred_element_type=jnp.float32).astype(
            jnp.bfloat16
        )
        forward_queries = projected[:, :model]
        forward_keys = projected[:, model : 2 * model]
        forward_values = projected[:, 2 * model :]
        forward_scores = attention_scores(
            forward_queries.reshape(length, heads, width),
            forward_keys.reshape(length, heads, width),
            segment,
        )
        peak = jnp.max(forward_scores, axis=-1, keepdims=True)
        raised = jnp.exp(forward_scores - peak)
        total = jnp.sum(raised, axis=-1, keepdims=True)
        forward_probs = raised / total
        log_total = peak + jnp.log(total)
        mixed = jnp.einsum(
            "hqk,khd->qhd",
            forward_probs.astype(jnp.bfloat16),
            forward_values.reshape(length, heads, width),
            preferred_element_type=jnp.float32,
        )
        mixed = mixed.reshape(length, model).astype(jnp.bfloat16)
        hidden = current + jnp.dot(mixed, output_w, preferred_element_type=jnp.float32)
        routed = normalize(hidden, gain_two).astype(jnp.bfloat16)
        chances = jax.nn.softmax(
            jnp.dot(routed, router_w, preferred_element_type=jnp.float32), axis=-1
        )
        forward_choose = (route[:, None] == expert_ids[None, :]).astype(jnp.float32)
        gate = jnp.sum(chances * forward_choose, axis=-1)
        target = route * capacity + slot
        spots = jnp.arange(experts * capacity, dtype=jnp.int32)
        place = (target[None, :] == spots[:, None]).astype(jnp.bfloat16)
        forward_outgoing = (
            jnp.dot(place, routed, preferred_element_type=jnp.float32)
            .astype(jnp.bfloat16)
            .reshape(owners, local * capacity, model)
        )
        arrived = lax.all_to_all(
            forward_outgoing, "expert", split_axis=0, concat_axis=0, tiled=True
        ).reshape(owners, local, capacity, model)
        before = jnp.einsum("secd,edf->secf", arrived, up_w, preferred_element_type=jnp.float32)
        activated, slope = gelu_both(before)
        activated, slope = lax.optimization_barrier((activated, slope))
        after = jnp.einsum(
            "secf,edf->secd", activated, down_w, preferred_element_type=jnp.float32
        ).astype(jnp.bfloat16)
        returned = lax.all_to_all(
            after.reshape(owners, local * capacity, model),
            "expert",
            split_axis=0,
            concat_axis=0,
            tiled=True,
        ).reshape(experts * capacity, model)
        forward_fetched = jnp.einsum(
            "sl,sd->ld", place, returned, preferred_element_type=jnp.float32
        ).astype(jnp.bfloat16)
        output = hidden + gate[:, None] * forward_fetched.astype(jnp.float32)
        forward_kept = {
            "inputs": inputs,
            "normed": forward_normed,
            "queries": forward_queries,
            "keys": forward_keys,
            "values": forward_values,
            "log_total": log_total,
            "mixed": mixed,
            "hidden": hidden,
            "routed": routed,
            "chances": chances,
            "gate": gate,
            "route": route,
            "place": place,
            "segment": segment,
            "arrived": arrived,
            "activated": activated,
            "slope": slope,
            "fetched": forward_fetched,
        }
        output, kept = (output, forward_kept)
        stash.append(kept)
        produced.append(output.astype(jnp.bfloat16))
        if tick < batches:
            received = from_behind(produced[-1], "section", 1)
    def pick(earlier, later):
        return earlier if earlier is later else jnp.where(first, earlier, later)

    steps = []
    arriving = jnp.zeros((length, model), jnp.bfloat16)
    results = []
    for tick in range(batches + 1):
        own = data[min(tick, batches - 1)]
        incoming = jnp.where(first, arriving, own).astype(jnp.float32)
        kept = jax.tree.map(pick, stash[max(tick - 1, 0)], stash[min(tick + 1, batches)])
        if tick == 0:
            kept = stash[min(1, batches)]
        elif tick == batches:
            kept = stash[batches - 1]
        grad_out = incoming
        fetched = kept["fetched"].astype(jnp.float32)
        gate_grad = jnp.sum(grad_out * fetched, axis=-1)
        weighted = (kept["gate"][:, None] * grad_out).astype(jnp.bfloat16)
        outgoing = (
            jnp.dot(kept["place"], weighted, preferred_element_type=jnp.float32)
            .astype(jnp.bfloat16)
            .reshape(owners, local * capacity, model)
        )
        arrived_grad = lax.all_to_all(
            outgoing, "expert", split_axis=0, concat_axis=0, tiled=True
        ).reshape(owners, local, capacity, model)
        activation_grad = jnp.einsum(
            "secd,edf->secf", arrived_grad, down_w, preferred_element_type=jnp.float32
        )
        before_grad = (activation_grad * kept["slope"].astype(jnp.float32)).astype(jnp.bfloat16)
        step = {
            "arrived": kept["arrived"],
            "activated": kept["activated"],
            "arrived_grad": arrived_grad,
            "before_grad": before_grad,
        }
        if tick == batches:
            steps.append(step)
            up_sum, down_sum = expert_sums(steps)
            up_sum, down_sum, before_grad = lax.optimization_barrier(
                (up_sum, down_sum, before_grad)
            )
            up_share = lax.psum_scatter(up_sum, "dp", scatter_dimension=1, tiled=True)
            down_share = lax.psum_scatter(down_sum, "dp", scatter_dimension=1, tiled=True)
        input_rows_grad = jnp.einsum(
            "secf,edf->secd", before_grad, up_w, preferred_element_type=jnp.float32
        ).astype(jnp.bfloat16)
        back_grad = lax.all_to_all(
            input_rows_grad.reshape(owners, local * capacity, model),
            "expert",
            split_axis=0,
            concat_axis=0,
            tiled=True,
        ).reshape(experts * capacity, model)
        routed_grad = jnp.einsum(
            "sl,sd->ld", kept["place"], back_grad, preferred_element_type=jnp.float32
        )
        choose = (kept["route"][:, None] == expert_ids[None, :]).astype(jnp.float32)
        logit_grad = kept["chances"] * (
            gate_grad[:, None] * choose - (gate_grad * kept["gate"])[:, None]
        )
        routed_full = kept["routed"].astype(jnp.float32)
        router_part = jnp.dot(routed_full.T, logit_grad, precision=highest)
        routed_grad = routed_grad + jnp.dot(
            logit_grad, router_w.astype(jnp.float32).T, precision=highest
        )
        second_pull = jax.vjp(normalize, kept["hidden"], gain_two)[1]
        hidden_part, gain_two_part = second_pull(routed_grad)
        hidden_grad = grad_out + hidden_part
        branch_grad = hidden_grad.astype(jnp.bfloat16)
        mixed_grad = (
            jnp.einsum("le,ce->lc", branch_grad, output_w, preferred_element_type=jnp.float32)
            .astype(jnp.bfloat16)
            .reshape(length, heads, width)
        )
        backward_queries = kept["queries"].reshape(length, heads, width)
        backward_keys = kept["keys"].reshape(length, heads, width)
        values = kept["values"].reshape(length, heads, width)
        probs = jnp.exp(
            attention_scores(backward_queries, backward_keys, kept["segment"]) - kept["log_total"]
        )
        prob_grad = jnp.einsum(
            "qhd,khd->hqk", mixed_grad, values, preferred_element_type=jnp.float32
        )
        value_grad = (
            jnp.einsum(
                "hqk,qhd->khd",
                probs.astype(jnp.bfloat16),
                mixed_grad,
                preferred_element_type=jnp.float32,
            )
            .astype(jnp.bfloat16)
            .reshape(length, model)
        )
        inner = jnp.sum(probs * prob_grad, axis=-1, keepdims=True)
        score_grad = (probs * (prob_grad - inner)).astype(jnp.bfloat16)
        query_grad = (
            (
                jnp.einsum(
                    "hqk,khd->qhd", score_grad, backward_keys, preferred_element_type=jnp.float32
                )
                * scale
            )
            .astype(jnp.bfloat16)
            .reshape(length, model)
        )
        key_grad = (
            (
                jnp.einsum(
                    "hqk,qhd->khd", score_grad, backward_queries, preferred_element_type=jnp.float32
                )
                * scale
            )
            .astype(jnp.bfloat16)
            .reshape(length, model)
        )
        projected_grad = jnp.concatenate([query_grad, key_grad, value_grad], 1)
        normed_grad = jnp.einsum(
            "le,ce->lc", projected_grad, qkv_w, preferred_element_type=jnp.float32
        )
        first_pull = jax.vjp(normalize, kept["inputs"].astype(jnp.float32), gain_one)[1]
        input_part, gain_one_part = first_pull(normed_grad)
        step["normed"] = kept["normed"]
        step["mixed"] = kept["mixed"]
        step["branch_grad"] = branch_grad
        step["projected_grad"] = projected_grad
        step["router"] = router_part
        step["gain_one"] = gain_one_part
        step["gain_two"] = gain_two_part
        step["score_grad"] = score_grad
        if tick < batches:
            steps.append(step)
        grad_in = hidden_grad + input_part
        results.append(grad_in.astype(jnp.bfloat16))
        if tick < batches:
            arriving = from_behind(results[-1], "section", -1)
    blocks = [jnp.where(first, results[index + 1], produced[index + 1]) for index in range(batches)]
    ends_out = jnp.concatenate(blocks, 0)[None]
    parts = merged(steps)
    score_sum = sum(part["score_grad"].astype(jnp.float32) for part in parts)
    table_sum = jnp.dot(bucket_hot, offset_sums(score_sum, length).T, precision=highest)
    projection_sum = jnp.concatenate(
        [
            product_sum(parts, "normed", "projected_grad", "lc,le->ce"),
            product_sum(parts, "mixed", "branch_grad", "lc,le->ce"),
        ],
        1,
    )
    shares = lax.all_gather(
        lax.psum_scatter(projection_sum, ("dp", "expert"), scatter_dimension=0, tiled=True),
        "expert",
        axis=0,
        tiled=True,
    ).astype(jnp.float32)
    small_sum = jnp.concatenate(
        [
            sum(part["gain_one"] for part in parts).reshape(layers, -1),
            sum(part["gain_two"] for part in parts).reshape(layers, -1),
            sum(part["router"] for part in parts).reshape(layers, -1),
            table_sum.reshape(layers, -1),
        ],
        1,
    ).astype(jnp.bfloat16)
    small_share = lax.dynamic_index_in_dim(
        lax.psum(small_sum, ("dp", "expert")), lax.axis_index("dp"), 0, keepdims=False
    ).astype(jnp.float32)
    return (
        ends_out,
        shares[None, :, :model],
        shares[None, :, model : 2 * model],
        shares[None, :, 2 * model : 3 * model],
        shares[None, :, 3 * model :],
        small_share[None, :rows],
        small_share[None, rows : 2 * rows],
        small_share[2 * rows : (2 + kinds) * rows].reshape(1, rows, kinds),
        small_share[(2 + kinds) * rows :].reshape(1, -1, bias_table.shape[2]),
        up_share.astype(jnp.float32)[None],
        jnp.swapaxes(down_share.astype(jnp.float32), 1, 2)[None],
    )


def solution(mesh):
    in_specs = (
        P("section", ("dp", "expert"), None),
        P("section", "dp", None),
        P("section", "dp", None),
        P("section", "dp", None),
        P("section", "dp", None),
        P("section", "dp"),
        P("section", "dp"),
        P("section", "dp", None),
        P("section", "dp", None),
        P("section", "expert", "dp", None),
        P("section", "expert", None, "dp"),
        P("section", ("dp", "expert")),
        P("section", ("dp", "expert")),
        P(("dp", "expert")),
        P(),
    )
    out_specs = (
        P("section", ("dp", "expert"), None),
        P("section", "dp", None),
        P("section", "dp", None),
        P("section", "dp", None),
        P("section", "dp", None),
        P("section", "dp"),
        P("section", "dp"),
        P("section", "dp", None),
        P("section", "dp", None),
        P("section", "expert", "dp", None),
        P("section", "expert", None, "dp"),
    )
    return jax.shard_map(shards, mesh=mesh, in_specs=in_specs, out_specs=out_specs, check_vma=False)
```

profile of v0, /device:TPU:0, one launch (start us, length us, event | category | flops | bytes accessed | tf_op | source)
XLA Modules:
  0.0 989.1 jit_solution(14753050407434140031)
XLA Ops:
  11.0 14.8 %all-gather = bf16[4,1,1248]{2,1,0:T(2,128)(2,1)S(1)} all-gather(bf16[1,1,1248]{2,1,0:T(2,128)(2,1)S(1)} %bitcast.473), channel_id=1, replica_groups=mesh['section'=2,'dp'=4,'expert'=4] {'dp'}, dimensions={0}, use_global_device_ids=true | all-gather | bytes 12480 | tf_op jit(solution)/shard_map/all_gather | solution.py:90
  26.8 3.4 broadcast_in_dim.73
  30.2 8.6 reshape.689
  38.8 4.2 concatenate.33
  43.0 4.9 copy.175
  50.6 20.7 %rev.6 = f32[12,256,256]{1,2,0:T(8,128)S(1)} reverse(f32[12,256,256]{1,2,0:T(8,128)} %copy.173), dimensions={2} | reverse | bytes 6291456 | tf_op jit(solution)/shard_map/rev | solution.py:34
  74.9 19.5 %all-gather.6.cloned.1.call-done = bf16[768,3072]{1,0:T(8,128)(2,1)} async-done(((bf16[48,3072]{1,0:T(8,128)(2,1)}), bf16[768,3072]{1,0:T(8,128)(2,1)}) %all-gather.6.cloned.1.call-update) | async-done | bytes 4718608 | tf_op jit(solution)/shard_map/all_gather | solution.py:82
  94.4 3.3 convolution_convert_fusion.2
  111.0 3.5 all-to-all-start
  114.5 69.5 %all-gather.8.cloned.1.call-done = bf16[1,1,768,3072]{3,2,1,0:T(8,128)(2,1)} async-done(((bf16[1,1,192,3072]{3,2,1,0:T(8,128)(2,1)}), bf16[1,1,768,3072]{3,2,1,0:T(8,128)(2,1)}) %all-gather.8.cloned.1.call-update) | async-done | bytes 4718608 | tf_op jit(solution)/shard_map/all_gather | solution.py:97
  184.1 8.3 fusion.8
  192.4 81.2 %all-gather.10.cloned.1.call-done = bf16[1,768,3072]{2,1,0:T(8,128)(2,1)} async-done(((bf16[1,192,3072]{2,1,0:T(8,128)(2,1)}), bf16[1,768,3072]{2,1,0:T(8,128)(2,1)}) %all-gather.10.cloned.1.call-update) | async-done | bytes 4718608 | tf_op jit(solution)/shard_map/all_gather | solution.py:98
  273.5 6.8 fusion.89
  280.3 3.8 all-to-all-start.1
  285.0 10.1 %all-to-all-done.1 = bf16[4,128,768]{2,1,0:T(8,128)(2,1)S(1)} async-done(((bf16[4,128,768]{2,1,0:T(8,128)(2,1)}), bf16[4,128,768]{2,1,0:T(8,128)(2,1)S(1)}, u32[]{:S(2)}, u32[]{:S(2)}) %all-to-all-start.1) | async-done | bytes 786464 | tf_op jit(solution)/shard_map/all_to_all | solution.py:202
  299.2 3.2 convolution_convert_fusion.1
  305.3 2.9 fusion.294
  315.1 4.2 all-to-all-start.3
  321.8 9.2 all-to-all-done.3
  331.0 4.2 all-to-all-start.2
  335.2 7.5 fusion.13
  344.4 5.9 fusion.94
  350.3 4.4 all-to-all-start.5
  354.8 6.2 fusion.2
  362.6 6.0 fusion.104
  368.6 4.2 all-to-all-start.4
  378.2 5.4 all-to-all-done.4
  383.7 3.2 multiply_reduce_fusion.3
  423.8 4.4 all-to-all-start.7
  428.2 5.1 fusion.139
  433.9 5.6 all-to-all-done.7
  439.4 7.5 fusion.18
  448.6 5.9 fusion.99
  454.5 4.3 all-to-all-start.9
  464.4 4.9 all-to-all-done.9
  475.1 4.2 all-to-all-start.6
  485.0 4.2 all-to-all-done.6
  489.3 6.2 fusion.55
  497.2 5.9 fusion.109
  503.1 4.5 all-to-all-start.8
  508.2 9.7 all-to-all-done.8
  547.0 4.6 all-to-all-start.10
  551.6 8.4 fusion.59
  560.1 5.2 fusion.166
  565.3 7.9 fusion.3
  573.2 5.5 fusion.54
  578.8 9.7 fusion.53
  588.4 6.9 fusion.112
  595.3 4.2 all-to-all-start.11
  599.7 5.7 fusion.172
  607.0 3.6 all-to-all-done.11
  631.2 3.8 add_convert_fusion
  641.2 4.6 fusion.138
  647.2 20.5 %rev.7 = f32[12,256,256]{1,2,0:T(8,128)S(1)} reverse(f32[12,256,256]{1,2,0:T(8,128)} %get-tuple-element.63), dimensions={2} | reverse | bytes 6291456 | tf_op jit(solution)/shard_map/rev | solution.py:39
  673.8 4.9 copy.176
  678.6 3.9 slice.189
  682.5 9.3 reshape.737
  691.8 3.7 reduce_sum.423
  696.0 72.8 %psum.7 = bf16[4,1248]{1,0:T(4,128)(2,1)} all-reduce(bf16[4,1248]{1,0:T(4,128)(2,1)S(1)} %concatenate.40), channel_id=1, replica_groups=mesh['section'=2,'dp'=4,'expert'=4] {'dp','expert'}, use_global_device_ids=true, to_apply=%region_43.44 | all-reduce | flops 4992 | bytes 19968 | tf_op jit(solution)/shard_map/psum | solution.py:402
  776.8 83.7 %reduce-scatter.6.cloned.1.call-done = bf16[1,192,3072]{2,1,0:T(8,128)(2,1)} async-done(((bf16[1,768,3072]{2,1,0:T(8,128)(2,1)}), bf16[1,192,3072]{2,1,0:T(8,128)(2,1)}) %reduce-scatter.6.cloned.1.call-update) | async-done | bytes 1179664 | tf_op jit(solution)/shard_map/reduce_scatter | solution.py:280
  860.5 2.9 bitcast_convert_fusion
  863.4 85.1 %reduce-scatter.8.cloned.1.call-done = bf16[1,192,3072]{2,1,0:T(8,128)(2,1)} async-done(((bf16[1,768,3072]{2,1,0:T(8,128)(2,1)}), bf16[1,192,3072]{2,1,0:T(8,128)(2,1)}) %reduce-scatter.8.cloned.1.call-update) | async-done | bytes 1179664 | tf_op jit(solution)/shard_map/reduce_scatter | solution.py:281
  948.5 2.9 convert_bitcast_fusion
  951.5 27.3 %all-gather.12.cloned.1.call-done = bf16[192,3072]{1,0:T(8,128)(2,1)} async-done(((bf16[48,3072]{1,0:T(8,128)(2,1)}), bf16[192,3072]{1,0:T(8,128)(2,1)}) %all-gather.12.cloned.1.call-update) | async-done | bytes 1179664 | tf_op jit(solution)/shard_map/all_gather | solution.py:386
  (541 shorter events, 183.6 us)
Async XLA Ops:
  7.2 19.4 %copy-start.148 = (s32[511]{0:T(512)S(1)}, s32[511]{0:T(512)}, u32[]{:S(2)}) copy-start(s32[511]{0:T(512)} %param.29) | copy-start | bytes 6136
  7.2 87.2 %all-gather.6.cloned.1.call-start = ((), (), s32[]{:S(2)}) async-start(), calls=%async_computation.15 | async-start | bytes 5013504 | tf_op jit(solution)/shard_map/all_gather | solution.py:82
  9.0 175.0 %all-gather.8.cloned.1.call-start = ((), (), s32[]{:S(2)}) async-start(), calls=%async_computation.16 | async-start | bytes 5898240 | tf_op jit(solution)/shard_map/all_gather | solution.py:97
  9.8 263.7 %all-gather.10.cloned.1.call-start = ((), (), s32[]{:S(2)}) async-start(), calls=%async_computation.17 | async-start | bytes 5898240 | tf_op jit(solution)/shard_map/all_gather | solution.py:98
  26.5 272.7 %copy-start.73 = (f32[768]{0:T(1024)}, f32[768]{0:T(1024)S(1)}, u32[]{:S(2)}) copy-start(f32[768]{0:T(1024)S(1)} %reshape.741) | copy-start | bytes 9220
  50.6 22.3 %copy-start.165 = (s32[512]{0:T(512)S(1)}, s32[512]{0:T(512)}, u32[]{:S(2)}) copy-start(s32[512]{0:T(512)} %param.28) | copy-start | bytes 6148
  50.6 22.9 %copy-start.162 = (s32[1,512]{1,0:T(1,128)S(1)}, s32[1,512]{1,0:T(1,128)}, u32[]{:S(2)}) copy-start(s32[1,512]{1,0:T(1,128)} %param.27) | copy-start | bytes 6148
  50.6 22.9 %copy-start.163 = (s32[1,512]{1,0:T(1,128)S(1)}, s32[1,512]{1,0:T(1,128)}, u32[]{:S(2)}) copy-start(s32[1,512]{1,0:T(1,128)} %param.26) | copy-start | bytes 6148
  71.3 32.4 %copy-start = (f32[12,256,256]{1,2,0:T(8,128)}, f32[12,256,256]{1,2,0:T(8,128)S(1)}, u32[]{:S(2)}) copy-start(f32[12,256,256]{1,2,0:T(8,128)S(1)} %rev.6) | copy-start | bytes 9437188
  71.4 312.2 %copy-start.76 = (f32[768]{0:T(1024)}, f32[768]{0:T(1024)S(1)}, u32[]{:S(2)}) copy-start(f32[768]{0:T(1024)S(1)} %reshape.742) | copy-start | bytes 9220
  72.9 24.8 %copy-start.124 = (f32[256]{0:T(256)}, f32[256]{0:T(256)S(1)}, u32[]{:S(2)}) copy-start(f32[256]{0:T(256)S(1)} %add_rsqrt_fusion.3) | copy-start | bytes 3076
  74.1 309.5 %copy-start.100 = (s32[1,256]{1,0:T(1,128)}, s32[1,256]{1,0:T(1,128)S(1)}, u32[]{:S(2)}) copy-start(s32[1,256]{1,0:T(1,128)S(1)} %get-tuple-element.115) | copy-start | bytes 3076
  109.6 185.5 %copy-start.26 = (f32[256,768]{1,0:T(8,128)}, f32[256,768]{1,0:T(8,128)S(1)}, u32[]{:S(2)}) copy-start(f32[256,768]{1,0:T(8,128)S(1)} %get-tuple-element.127) | copy-start | bytes 2359300
  109.8 174.9 %copy-start.42 = (bf16[256,768]{1,0:T(8,128)(2,1)}, bf16[256,768]{1,0:T(8,128)(2,1)S(1)}, u32[]{:S(2)}) copy-start(bf16[256,768]{1,0:T(8,128)(2,1)S(1)} %multiply_convert_fusion.5) | copy-start | bytes 1179652
  111.0 73.0 %all-to-all-start = ((bf16[4,128,768]{2,1,0:T(8,128)(2,1)}), bf16[4,128,768]{2,1,0:T(8,128)(2,1)S(1)}, u32[]{:S(2)}, u32[]{:S(2)}) async-start(bf16[4,128,768]{2,1,0:T(8,128)(2,1)} %bitcast.17), calls=%async_computation | async-start | bytes 1572864 | tf_op jit(solution)/shard_map/all_to_all | solution.py:193
  192.4 91.8 %copy-start.94 = (bf16[4,1,1248]{2,0,1:T(4,128)(2,1)S(1)}, bf16[4,1,1248]{2,0,1:T(4,128)(2,1)}, u32[]{:S(2)}) copy-start(bf16[4,1,1248]{2,0,1:T(4,128)(2,1)} %copy-done.93) | copy-start | bytes 29956
  192.4 92.6 %copy-start.141 = (s32[1,256]{1,0:T(1,128)S(1)}, s32[1,256]{1,0:T(1,128)}, u32[]{:S(2)}) copy-start(s32[1,256]{1,0:T(1,128)} %get-tuple-element.122) | copy-start | bytes 3076
  280.3 17.5 %copy-start.139 = (s32[1,256]{1,0:T(1,128)S(1)}, s32[1,256]{1,0:T(1,128)}, u32[]{:S(2)}) copy-start(s32[1,256]{1,0:T(1,128)} %get-tuple-element.123) | copy-start | bytes 3076
  280.3 14.8 %all-to-all-start.1 = ((bf16[4,128,768]{2,1,0:T(8,128)(2,1)}), bf16[4,128,768]{2,1,0:T(8,128)(2,1)S(1)}, u32[]{:S(2)}, u32[]{:S(2)}) async-start(bf16[4,128,768]{2,1,0:T(8,128)(2,1)} %fusion.89), calls=%async_computation.1 | async-start | bytes 1572864 | tf_op jit(solution)/shard_map/all_to_all | solution.py:202
  284.9 12.9 %copy-start.113 = (f32[256]{0:T(256)}, f32[256]{0:T(256)S(1)}, u32[]{:S(2)}) copy-start(f32[256]{0:T(256)S(1)} %get-tuple-element.128) | copy-start | bytes 3076
  284.9 234.7 %copy-start.89 = (f32[256,4]{0,1:T(4,128)}, f32[256,4]{0,1:T(4,128)S(1)}, u32[]{:S(2)}) copy-start(f32[256,4]{0,1:T(4,128)S(1)} %get-tuple-element.129) | copy-start | bytes 12292
  284.9 14.2 %copy-start.131 = (f32[256]{0:T(256)}, f32[256]{0:T(256)S(1)}, u32[]{:S(2)}) copy-start(f32[256]{0:T(256)S(1)} %fusion.239) | copy-start | bytes 3076
  285.0 13.5 %copy-start.137 = (f32[256]{0:T(256)}, f32[256]{0:T(256)S(1)}, u32[]{:S(2)}) copy-start(f32[256]{0:T(256)S(1)} %select_reduce_fusion.2) | copy-start | bytes 3076
  296.3 2.6 collective-permute-start
  298.4 77.8 %copy-start.95 = (s32[256]{0:T(256)}, s32[256]{0:T(256)S(1)}, u32[]{:S(2)}) copy-start(s32[256]{0:T(256)S(1)} %get-tuple-element.121) | copy-start | bytes 3076
  312.2 77.8 %copy-start.98 = (f32[256]{0:T(256)}, f32[256]{0:T(256)S(1)}, u32[]{:S(2)}) copy-start(f32[256]{0:T(256)S(1)} %fusion.266) | copy-start | bytes 3076
  315.1 15.9 %all-to-all-start.3 = ((bf16[4,128,768]{2,1,0:T(8,128)(2,1)}), bf16[4,128,768]{2,1,0:T(8,128)(2,1)}, u32[]{:S(2)}, u32[]{:S(2)}) async-start(bf16[4,128,768]{2,1,0:T(8,128)(2,1)} %bitcast.420), calls=%async_computation.3 | async-start | bytes 1572864 | tf_op jit(solution)/shard_map/all_to_all | solution.py:193
  319.4 64.3 %copy-start.105 = (f32[256]{0:T(256)}, f32[256]{0:T(256)S(1)}, u32[]{:S(2)}) copy-start(f32[256]{0:T(256)S(1)} %get-tuple-element.80) | copy-start | bytes 3076
  319.4 286.1 %copy-start.87 = (f32[256,4]{0,1:T(4,128)}, f32[256,4]{0,1:T(4,128)S(1)}, u32[]{:S(2)}) copy-start(f32[256,4]{0,1:T(4,128)S(1)} %get-tuple-element.81) | copy-start | bytes 12292
  331.0 19.3 %all-to-all-start.2 = ((bf16[4,128,768]{2,1,0:T(8,128)(2,1)}), bf16[4,128,768]{2,1,0:T(8,128)(2,1)}, u32[]{:S(2)}, u32[]{:S(2)}) async-start(bf16[4,128,768]{2,1,0:T(8,128)(2,1)} %bitcast.450), calls=%async_computation.2 | async-start | bytes 1572864 | tf_op jit(solution)/shard_map/all_to_all | solution.py:261
  350.3 18.3 %all-to-all-start.5 = ((bf16[4,128,768]{2,1,0:T(8,128)(2,1)}), bf16[4,128,768]{2,1,0:T(8,128)(2,1)}, u32[]{:S(2)}, u32[]{:S(2)}) async-start(bf16[4,128,768]{2,1,0:T(8,128)(2,1)} %fusion.94), calls=%async_computation.5 | async-start | bytes 1572864 | tf_op jit(solution)/shard_map/all_to_all | solution.py:202
  368.6 15.1 %all-to-all-start.4 = ((bf16[4,128,768]{2,1,0:T(8,128)(2,1)}), bf16[4,128,768]{2,1,0:T(8,128)(2,1)}, u32[]{:S(2)}, u32[]{:S(2)}) async-start(bf16[4,128,768]{2,1,0:T(8,128)(2,1)} %fusion.104), calls=%async_computation.4 | async-start | bytes 1572864 | tf_op jit(solution)/shard_map/all_to_all | solution.py:285
  386.9 3.0 collective-permute-start.2
  423.8 15.6 %all-to-all-start.7 = ((bf16[4,128,768]{2,1,0:T(8,128)(2,1)}), bf16[4,128,768]{2,1,0:T(8,128)(2,1)}, u32[]{:S(2)}, u32[]{:S(2)}) async-start(bf16[4,128,768]{2,1,0:T(8,128)(2,1)} %bitcast.421), calls=%async_computation.7 | async-start | bytes 1572864 | tf_op jit(solution)/shard_map/all_to_all | solution.py:193
  454.5 14.8 %all-to-all-start.9 = ((bf16[4,128,768]{2,1,0:T(8,128)(2,1)}), bf16[4,128,768]{2,1,0:T(8,128)(2,1)}, u32[]{:S(2)}, u32[]{:S(2)}) async-start(bf16[4,128,768]{2,1,0:T(8,128)(2,1)} %fusion.99), calls=%async_computation.9 | async-start | bytes 1572864 | tf_op jit(solution)/shard_map/all_to_all | solution.py:202
  458.9 13.1 %copy-start.138 = (f32[256]{0:T(256)S(1)}, f32[256]{0:T(256)}, u32[]{:S(2)}) copy-start(f32[256]{0:T(256)} %copy-done.137) | copy-start | bytes 3076
  458.9 13.7 %copy-start.143 = (s32[1,256]{1,0:T(1,128)S(1)}, s32[1,256]{1,0:T(1,128)}, u32[]{:S(2)}) copy-start(s32[1,256]{1,0:T(1,128)} %get-tuple-element.114) | copy-start | bytes 3076
  460.6 3.7 collective-permute-start.1
  463.2 56.4 %copy-start.91 = (f32[256,4]{0,1:T(4,128)}, f32[256,4]{0,1:T(4,128)S(1)}, u32[]{:S(2)}) copy-start(f32[256,4]{0,1:T(4,128)S(1)} %get-tuple-element.151) | copy-start | bytes 12292
  463.2 56.4 %copy-start.116 = (f32[256]{0:T(256)}, f32[256]{0:T(256)S(1)}, u32[]{:S(2)}) copy-start(f32[256]{0:T(256)S(1)} %get-tuple-element.150) | copy-start | bytes 3076
  463.3 56.4 %copy-start.135 = (f32[256]{0:T(256)}, f32[256]{0:T(256)S(1)}, u32[]{:S(2)}) copy-start(f32[256]{0:T(256)S(1)} %fusion.243) | copy-start | bytes 3076
  463.3 11.8 %copy-start.134 = (f32[256]{0:T(256)}, f32[256]{0:T(256)S(1)}, u32[]{:S(2)}) copy-start(f32[256]{0:T(256)S(1)} %select_reduce_fusion) | copy-start | bytes 3076
  472.0 23.4 %copy-start.152 = (f32[256]{0:T(256)}, f32[256]{0:T(256)S(1)}, u32[]{:S(2)}) copy-start(f32[256]{0:T(256)S(1)} %get-tuple-element.148) | copy-start | bytes 3076
  475.1 14.2 %all-to-all-start.6 = ((bf16[4,128,768]{2,1,0:T(8,128)(2,1)}), bf16[4,128,768]{2,1,0:T(8,128)(2,1)}, u32[]{:S(2)}, u32[]{:S(2)}) async-start(bf16[4,128,768]{2,1,0:T(8,128)(2,1)} %bitcast.451), calls=%async_computation.6 | async-start | bytes 1572864 | tf_op jit(solution)/shard_map/all_to_all | solution.py:261
  503.1 16.6 %copy-start.114 = (f32[256]{0:T(256)S(1)}, f32[256]{0:T(256)}, u32[]{:S(2)}) copy-start(f32[256]{0:T(256)} %copy-done.113) | copy-start | bytes 3076
  503.1 16.6 %copy-start.132 = (f32[256]{0:T(256)S(1)}, f32[256]{0:T(256)}, u32[]{:S(2)}) copy-start(f32[256]{0:T(256)} %copy-done.131) | copy-start | bytes 3076
  503.1 14.9 %all-to-all-start.8 = ((bf16[4,128,768]{2,1,0:T(8,128)(2,1)}), bf16[4,128,768]{2,1,0:T(8,128)(2,1)}, u32[]{:S(2)}, u32[]{:S(2)}) async-start(bf16[4,128,768]{2,1,0:T(8,128)(2,1)} %fusion.109), calls=%async_computation.8 | async-start | bytes 1572864 | tf_op jit(solution)/shard_map/all_to_all | solution.py:285
  538.2 5.2 collective-permute-start.3
  544.9 60.6 %copy-start.108 = (f32[256]{0:T(256)}, f32[256]{0:T(256)S(1)}, u32[]{:S(2)}) copy-start(f32[256]{0:T(256)S(1)} %get-tuple-element.67) | copy-start | bytes 3076
  547.0 18.3 %all-to-all-start.10 = ((bf16[4,128,768]{2,1,0:T(8,128)(2,1)}), bf16[4,128,768]{2,1,0:T(8,128)(2,1)}, u32[]{:S(2)}, u32[]{:S(2)}) async-start(bf16[4,128,768]{2,1,0:T(8,128)(2,1)} %bitcast.418), calls=%async_computation.10 | async-start | bytes 1572864 | tf_op jit(solution)/shard_map/all_to_all | solution.py:261
  588.4 11.3 %copy-start.125 = (f32[256]{0:T(256)S(1)}, f32[256]{0:T(256)}, u32[]{:S(2)}) copy-start(f32[256]{0:T(256)} %copy-done.124) | copy-start | bytes 3076
  588.4 11.3 %copy-start.127 = (f32[256]{0:T(256)S(1)}, f32[256]{0:T(256)}, u32[]{:S(2)}) copy-start(f32[256]{0:T(256)} %copy-done.126) | copy-start | bytes 3076
  595.3 15.4 %all-to-all-start.11 = ((bf16[4,128,768]{2,1,0:T(8,128)(2,1)}), bf16[4,128,768]{2,1,0:T(8,128)(2,1)}, u32[]{:S(2)}, u32[]{:S(2)}) async-start(bf16[4,128,768]{2,1,0:T(8,128)(2,1)} %fusion.112), calls=%async_computation.11 | async-start | bytes 1572864 | tf_op jit(solution)/shard_map/all_to_all | solution.py:285
  599.5 11.2 %copy-start.99 = (f32[256]{0:T(256)S(1)}, f32[256]{0:T(256)}, u32[]{:S(2)}) copy-start(f32[256]{0:T(256)} %copy-done.98) | copy-start | bytes 3076
  599.5 174.4 %reduce-scatter.4.cloned.1.call-start = ((), (), s32[]{:S(2)}) async-start(), calls=%async_computation.18 | async-start | bytes 5013504 | tf_op jit(solution)/shard_map/reduce_scatter | solution.py:387
  638.0 222.5 %reduce-scatter.6.cloned.1.call-start = ((), (), s32[]{:S(2)}) async-start(), calls=%async_computation.20 | async-start | bytes 5898240 | tf_op jit(solution)/shard_map/reduce_scatter | solution.py:280
  638.8 309.8 %reduce-scatter.8.cloned.1.call-start = ((), (), s32[]{:S(2)}) async-start(), calls=%async_computation.21 | async-start | bytes 5898240 | tf_op jit(solution)/shard_map/reduce_scatter | solution.py:281
  639.3 339.5 %all-gather.12.cloned.1.call-start = ((), (), s32[]{:S(2)}) async-start(), calls=%async_computation.19 | async-start | bytes 1474560 | tf_op jit(solution)/shard_map/all_gather | solution.py:386
  691.8 77.0 %copy-start.155 = (f32[256]{0:T(256)S(1)}, f32[256]{0:T(256)}, u32[]{:S(2)}) copy-start(f32[256]{0:T(256)} %get-tuple-element.77) | copy-start | bytes 3076
  691.8 77.0 %copy-start.166 = (f32[256]{0:T(256)S(1)}, f32[256]{0:T(256)}, u32[]{:S(2)}) copy-start(f32[256]{0:T(256)} %get-tuple-element.60) | copy-start | bytes 3076
  691.8 77.0 %copy-start.11 = (f32[256,768]{1,0:T(8,128)S(1)}, f32[256,768]{1,0:T(8,128)}, u32[]{:S(2)}) copy-start(f32[256,768]{1,0:T(8,128)} %copy-done.9) | copy-start | bytes 2359300
  691.8 77.0 %copy-start.56 = (f32[256,768]{1,0:T(8,128)S(1)}, f32[256,768]{1,0:T(8,128)}, u32[]{:S(2)}) copy-start(f32[256,768]{1,0:T(8,128)} %copy-done.55) | copy-start | bytes 2359300
  691.8 77.0 %copy-start.72 = (f32[256,768]{1,0:T(8,128)S(1)}, f32[256,768]{1,0:T(8,128)}, u32[]{:S(2)}) copy-start(f32[256,768]{1,0:T(8,128)} %get-tuple-element.159) | copy-start | bytes 2359300
  695.5 74.7 %copy-start.64 = (bf16[256,768]{1,0:T(8,128)(2,1)S(1)}, bf16[256,768]{1,0:T(8,128)(2,1)}, u32[]{:S(2)}) copy-start(bf16[256,768]{1,0:T(8,128)(2,1)} %get-tuple-element.65) | copy-start | bytes 1179652
  (136 other events, 434.3 us)
Sparse Core Ops, SparseCore 0:
  11.4 82.9 all-gather.5
  96.0 88.0 all-gather.7
  185.6 87.8 all-gather.9
  638.1 135.7 reduce-scatter.3
  776.1 84.3 reduce-scatter.5
  862.7 85.7 reduce-scatter.7
  950.5 28.2 all-gather.11
where the time goes:
time: 1000 us; the launch traced here: 989 us
  waiting for transfers between devices  426 us (43%)
  matrix products  209 us (21%)
  local copies, waits for them, and re-layouts  148 us (15%)
  blocking collectives  87.6 us (9%)
  starting transfers between devices  57 us (6%)
  other arithmetic  45.1 us (5%)
  between operations  16.7 us (2%)
    reduce_scatter x1, waiting for transfers between devices, shards(): lax.psum_scatter(down_sum, 'dp', scatter_dimension=1, tiled=True)  85.1 us
    reduce_scatter x1, waiting for transfers between devices, shards(): up_share = lax.psum_scatter(up_sum, 'dp', scatter_dimension=1, tiled=True)  83.7 us
    all_gather x1, waiting for transfers between devices, shards(): lax.all_gather(jnp.swapaxes(experts_down[0], 1, 2), 'dp', axis=1, tiled=T...  81.2 us
    psum x1, blocking collectives, shards(): lax.psum(small_sum, ('dp', 'expert'))  72.8 us
    all_gather x1, waiting for transfers between devices, shards(): up_w = lax.all_gather(experts_up, 'dp', axis=2, tiled=True)[0]  69.5 us
    dot_general x8, matrix products, product_sum(): jnp.einsum(form, part[left], part[right], preferred_element_type=jnp.floa...  39.4 us
    unnamed x362, local copies, waits for them, and re-layouts  38.9 us
    all_gather x1, waiting for transfers between devices, shards(): lax.all_gather(lax.psum_scatter(projection_sum, ('dp', 'expert'), scatter...  27.3 us
  transfers between devices with their start and end apart: 23, of which 17 were waited for; matrix products, arithmetic and copies ran while one was open for 22% of the time, Pallas kernels for 0%

commit v1 on v0

v1 whole, which is shorter than its diff:
```python
import functools
from typing import NamedTuple

import jax
import jax.numpy as jnp
from jax import lax
from jax.experimental import pallas as pl
from jax.experimental.pallas import tpu as pltpu
from jax.sharding import PartitionSpec as P

SECTION, DP, EXPERT = "section", "dp", "expert"
epsilon = 1e-06
highest = lax.Precision.HIGHEST


class Kept(NamedTuple):
    inputs: jax.Array
    normed: jax.Array
    projected: jax.Array
    mixed: jax.Array
    hidden: jax.Array
    routed: jax.Array
    chances: jax.Array
    gate: jax.Array
    route: jax.Array
    place: jax.Array
    segment: jax.Array
    arrived: jax.Array
    activated: jax.Array
    slope: jax.Array
    fetched: jax.Array


class ExpertStep(NamedTuple):
    arrived: jax.Array
    activated: jax.Array
    arrived_grad: jax.Array
    before_grad: jax.Array


class SharedStep(NamedTuple):
    normed: jax.Array
    mixed: jax.Array
    branch_grad: jax.Array
    projected_grad: jax.Array
    router: jax.Array
    gain_one: jax.Array
    gain_two: jax.Array
    score_grad: jax.Array


def from_behind(value, axis, steps):
    count = lax.axis_size(axis)
    first, last = (max(0, -steps), min(count, count - steps))
    return lax.ppermute(value, axis, [(source, source + steps) for source in range(first, last)])


def normalize(values, gain):
    return values * lax.rsqrt(jnp.mean(values * values, axis=-1, keepdims=True) + epsilon) * gain


def gelu_both(values):
    below = 0.5 * (1.0 + lax.erf(values * (0.5**0.5)))
    density = jnp.exp(-0.5 * values * values) * ((2.0 * jnp.pi) ** -0.5)
    return (values * below).astype(jnp.bfloat16), (below + values * density).astype(jnp.bfloat16)


def head_scores(query, key, bias, same):
    scores = lax.dot_general(
        query, key, (((1,), (1,)), ((), ())), preferred_element_type=jnp.float32
    )
    scores = jnp.where(same, scores * (query.shape[1] ** -0.5) + bias, -1e30)
    raised = jnp.exp(scores - jnp.max(scores, axis=-1, keepdims=True))
    return raised / jnp.sum(raised, axis=-1, keepdims=True)


def forward_body(width, column, row, query, key, value, bias, mixed):
    same = column[...] == row[...]
    parts = []
    for head in range(bias.shape[0]):
        lanes = slice(head * width, (head + 1) * width)
        probs = head_scores(query[:, lanes], key[:, lanes], bias[head], same)
        parts.append(
            jnp.dot(
                probs.astype(jnp.bfloat16), value[:, lanes], preferred_element_type=jnp.float32
            )
        )
    mixed[...] = jnp.concatenate(parts, 1).astype(jnp.bfloat16)


def backward_body(
    width, column, row, query, key, value, mixed, bias, query_out, key_out, value_out, score_out
):
    same = column[...] == row[...]
    scale = width**-0.5
    rows = (((0,), (0,)), ((), ()))
    columns = (((1,), (1,)), ((), ()))
    query_parts, key_parts, value_parts = [], [], []
    for head in range(bias.shape[0]):
        lanes = slice(head * width, (head + 1) * width)
        own_query, own_key, grad = query[:, lanes], key[:, lanes], mixed[:, lanes]
        probs = head_scores(own_query, own_key, bias[head], same)
        prob_grad = lax.dot_general(
            grad, value[:, lanes], columns, preferred_element_type=jnp.float32
        )
        value_parts.append(
            lax.dot_general(
                probs.astype(jnp.bfloat16), grad, rows, preferred_element_type=jnp.float32
            )
        )
        inner = jnp.sum(probs * prob_grad, axis=-1, keepdims=True)
        score_grad = (probs * (prob_grad - inner)).astype(jnp.bfloat16)
        score_out[head] = score_grad
        query_parts.append(jnp.dot(score_grad, own_key, preferred_element_type=jnp.float32))
        key_parts.append(
            lax.dot_general(score_grad, own_query, rows, preferred_element_type=jnp.float32)
        )
    query_out[...] = (jnp.concatenate(query_parts, 1) * scale).astype(jnp.bfloat16)
    key_out[...] = (jnp.concatenate(key_parts, 1) * scale).astype(jnp.bfloat16)
    value_out[...] = jnp.concatenate(value_parts, 1).astype(jnp.bfloat16)


def spread_body(rows, relative):
    length = relative.shape[1]
    wide = jnp.broadcast_to(rows[0], (length, 2 * length))
    relative[0] = pltpu.roll(wide, 0, 1, stride=1, stride_axis=0)[:, :length]


def offset_body(one, two, sums):
    length = one.shape[1]
    down = lax.broadcasted_iota(jnp.int32, (length, length), 0)
    across = lax.broadcasted_iota(jnp.int32, (length, length), 1)
    turn = (down + across == length - 1).astype(jnp.bfloat16)
    turned = jnp.dot(one[0], turn, preferred_element_type=jnp.float32) + jnp.dot(
        two[0], turn, preferred_element_type=jnp.float32
    )
    wide = jnp.concatenate([turned, jnp.zeros((length, length), jnp.float32)], 1)
    sums[0] = jnp.sum(
        pltpu.roll(wide, 0, 1, stride=1, stride_axis=0), axis=0, keepdims=True
    )


def attention_specs(length, heads, width):
    group = 2 if heads % 2 == 0 else heads
    groups = heads // group
    line = pl.BlockSpec((length, 1), lambda step: (0, 0))
    flat = pl.BlockSpec((1, length), lambda step: (0, 0))
    blocks = [
        pl.BlockSpec((length, group * width), lambda step, shift=shift: (0, step + shift * groups))
        for shift in range(3)
    ]
    square = pl.BlockSpec((group, length, length), lambda step: (step, 0, 0))
    return groups, line, flat, blocks, square


roomy = 40 * 1024 * 1024


def attend(projected, relative, segment):
    heads, length, _ = relative.shape
    model = projected.shape[1] // 3
    groups, line, flat, blocks, square = attention_specs(length, heads, model // heads)
    return pl.pallas_call(
        functools.partial(forward_body, model // heads),
        grid=(groups,),
        in_specs=[line, flat, *blocks, square],
        out_specs=blocks[0],
        out_shape=jax.ShapeDtypeStruct((length, model), jnp.bfloat16),
        compiler_params=pltpu.CompilerParams(vmem_limit_bytes=roomy),
        name="attend",
    )(segment[:, None], segment[None, :], projected, projected, projected, relative)


def attend_back(projected, mixed_grad, relative, segment):
    heads, length, _ = relative.shape
    model = projected.shape[1] // 3
    groups, line, flat, blocks, square = attention_specs(length, heads, model // heads)
    piece = jax.ShapeDtypeStruct((length, model), jnp.bfloat16)
    return pl.pallas_call(
        functools.partial(backward_body, model // heads),
        grid=(groups,),
        in_specs=[line, flat, *blocks, blocks[0], square],
        out_specs=[blocks[0], blocks[0], blocks[0], square],
        out_shape=[piece, piece, piece, jax.ShapeDtypeStruct(relative.shape, jnp.bfloat16)],
        compiler_params=pltpu.CompilerParams(vmem_limit_bytes=roomy),
        name="attend_back",
    )(segment[:, None], segment[None, :], projected, projected, projected, mixed_grad, relative)


def spread_offsets(rows, length):
    heads = rows.shape[0]
    return pl.pallas_call(
        spread_body,
        grid=(heads,),
        in_specs=[pl.BlockSpec((1, 1, 2 * length), lambda head: (head, 0, 0))],
        out_specs=pl.BlockSpec((1, length, length), lambda head: (head, 0, 0)),
        out_shape=jax.ShapeDtypeStruct((heads, length, length), jnp.float32),
        name="spread_offsets",
    )(rows[:, None, :])


def offset_sums(one, two):
    heads, length, _ = one.shape
    square = pl.BlockSpec((1, length, length), lambda head: (head, 0, 0))
    return pl.pallas_call(
        offset_body,
        grid=(heads,),
        in_specs=[square, square],
        out_specs=pl.BlockSpec((1, 1, 2 * length), lambda head: (head, 0, 0)),
        out_shape=jax.ShapeDtypeStruct((heads, 1, 2 * length), jnp.float32),
        name="offset_sums",
    )(one, two)[:, 0, : 2 * length - 1]


def shards(
    ends,
    w_query,
    w_key,
    w_value,
    w_output,
    gain_attention,
    gain_experts,
    router,
    bias_table,
    experts_up,
    experts_down,
    routes,
    slots,
    segments,
    buckets,
):
    section = lax.axis_index(SECTION)
    first = section == 0
    length = (buckets.shape[0] + 1) // 2
    model = ends.shape[2]
    batches = ends.shape[1] // length
    owners = lax.axis_size(EXPERT)
    layers = lax.axis_size(DP)
    mine = lax.axis_index(EXPERT)
    projections = jnp.concatenate([w_query[0], w_key[0], w_value[0], w_output[0]], 1)
    piece = projections.shape[0] // owners
    small = jnp.concatenate(
        [
            gain_attention.reshape(1, -1),
            gain_experts.reshape(1, -1),
            router.reshape(1, -1),
            bias_table.reshape(1, -1),
        ],
        1,
    )
    quarter = lax.all_gather(
        lax.dynamic_slice_in_dim(projections, mine * piece, piece, 0), DP, axis=0
    )

    def spread(block):
        return lax.all_to_all(
            jnp.broadcast_to(block[None], (owners, *block.shape)),
            EXPERT,
            split_axis=0,
            concat_axis=0,
            tiled=True,
        )

    small = lax.all_gather(small, DP, axis=0, tiled=True)
    rows = w_query.shape[1]
    kinds = router.shape[2]
    gain_one = small[:, :rows].reshape(-1).astype(jnp.float32)
    gain_two = small[:, rows : 2 * rows].reshape(-1).astype(jnp.float32)
    router_w = small[:, 2 * rows : (2 + kinds) * rows].reshape(-1, kinds)
    table = small[:, (2 + kinds) * rows :].reshape(-1, bias_table.shape[2]).astype(jnp.float32)
    own_up = experts_up[0]
    own_down = jnp.swapaxes(experts_down[0], 1, 2)
    swapped = lax.ppermute(jnp.where(first, own_down, own_up), SECTION, [(0, 1), (1, 0)])
    own_up, own_down, swapped, quarter = lax.optimization_barrier(
        (own_up, own_down, swapped, quarter)
    )
    early_w = lax.all_gather(jnp.where(first, own_up, swapped), DP, axis=1, tiled=True)
    late_w = lax.all_gather(jnp.where(first, swapped, own_down), DP, axis=1, tiled=True)
    early_down = lax.ppermute(early_w, SECTION, [(1, 0)])
    late_up = lax.ppermute(late_w, SECTION, [(0, 1)])
    up_w = jnp.where(first, early_w, late_up)
    down_w = jnp.where(first, early_down, late_w)
    gathered = jnp.swapaxes(spread(quarter), 0, 1).reshape(layers * owners * piece, -1)
    qkv_w = gathered[:, : 3 * model]
    output_w = gathered[:, 3 * model :]
    local = up_w.shape[0]
    experts = owners * local
    capacity = 2 * length // experts
    heads = table.shape[1]
    bucket_hot = (buckets[None, :] == jnp.arange(table.shape[0], dtype=jnp.int32)[:, None]).astype(
        jnp.float32
    )
    backwards = jnp.concatenate(
        [buckets[:length][::-1], jnp.full((1,), -1, jnp.int32), buckets[length:][::-1]]
    )
    backwards_hot = (
        backwards[None, :] == jnp.arange(table.shape[0], dtype=jnp.int32)[:, None]
    ).astype(jnp.float32)
    relative = spread_offsets(jnp.dot(table.T, backwards_hot, precision=highest), length)
    my_routes = routes[0].reshape(batches, length)
    my_slots = slots[0].reshape(batches, length)
    my_segments = segments.reshape(batches, length)
    data = ends[0].reshape(batches, length, model)
    expert_ids = jnp.arange(experts, dtype=jnp.int32)

    def merged(all_steps):
        ends_step = jax.tree.map(pick, all_steps[batches], all_steps[0])
        return all_steps[1:batches] + [ends_step]

    def product(lefts, rights):
        return lax.dot_general(
            jnp.concatenate(lefts, 0),
            jnp.concatenate(rights, 0),
            (((0,), (0,)), ((), ())),
            preferred_element_type=jnp.float32,
        ).astype(jnp.bfloat16)

    def expert_product(lefts, rights):
        return jnp.stack(
            [
                product(
                    [left[:, one].reshape(-1, left.shape[3]) for left in lefts],
                    [right[:, one].reshape(-1, right.shape[3]) for right in rights],
                )
                for one in range(local)
            ]
        )

    def later_sums(*all_steps):
        return (
            expert_product(
                [each.arrived for each in all_steps], [each.before_grad for each in all_steps]
            ),
            expert_product(
                [each.arrived_grad for each in all_steps], [each.activated for each in all_steps]
            ),
        )

    def empty_sums(*all_steps):
        shape = up_w.shape
        return jnp.zeros(shape, jnp.bfloat16), jnp.zeros(shape, jnp.bfloat16)

    received = jnp.zeros((length, model), jnp.bfloat16)
    stash = []
    produced = []
    for tick in range(batches + 1):
        early = min(tick, batches - 1)
        late = max(tick - 1, 0)
        inputs = jnp.where(first, data[early], received)
        route = jnp.where(first, my_routes[early], my_routes[late])
        slot = jnp.where(first, my_slots[early], my_slots[late])
        segment = jnp.where(first, my_segments[early], my_segments[late])
        current = inputs.astype(jnp.float32)
        forward_normed = normalize(current, gain_one).astype(jnp.bfloat16)
        projected = jnp.dot(forward_normed, qkv_w, preferred_element_type=jnp.float32).astype(
            jnp.bfloat16
        )
        mixed = attend(projected, relative, segment)
        hidden = current + jnp.dot(mixed, output_w, preferred_element_type=jnp.float32)
        routed = normalize(hidden, gain_two).astype(jnp.bfloat16)
        chances = jax.nn.softmax(
            jnp.dot(routed, router_w, preferred_element_type=jnp.float32), axis=-1
        )
        forward_choose = (route[:, None] == expert_ids[None, :]).astype(jnp.float32)
        gate = jnp.sum(chances * forward_choose, axis=-1)
        target = route * capacity + slot
        spots = jnp.arange(experts * capacity, dtype=jnp.int32)
        place = (target[None, :] == spots[:, None]).astype(jnp.bfloat16)
        forward_outgoing = (
            jnp.dot(place, routed, preferred_element_type=jnp.float32)
            .astype(jnp.bfloat16)
            .reshape(owners, local * capacity, model)
        )
        arrived = lax.all_to_all(
            forward_outgoing, EXPERT, split_axis=0, concat_axis=0, tiled=True
        ).reshape(owners, local, capacity, model)
        tick_up, tick_down = (early_w, early_down) if tick == 0 else (up_w, down_w)
        before = jnp.einsum("secd,edf->secf", arrived, tick_up, preferred_element_type=jnp.float32)
        activated, slope = gelu_both(before)
        activated, slope = lax.optimization_barrier((activated, slope))
        after = jnp.einsum(
            "secf,edf->secd", activated, tick_down, preferred_element_type=jnp.float32
        ).astype(jnp.bfloat16)
        returned = lax.all_to_all(
            after.reshape(owners, local * capacity, model),
            EXPERT,
            split_axis=0,
            concat_axis=0,
            tiled=True,
        ).reshape(experts * capacity, model)
        forward_fetched = jnp.einsum(
            "sl,sd->ld", place, returned, preferred_element_type=jnp.float32
        ).astype(jnp.bfloat16)
        output = hidden + gate[:, None] * forward_fetched.astype(jnp.float32)
        forward_kept = Kept(
            inputs=inputs,
            normed=forward_normed,
            projected=projected,
            mixed=mixed,
            hidden=hidden,
            routed=routed,
            chances=chances,
            gate=gate,
            route=route,
            place=place,
            segment=segment,
            arrived=arrived,
            activated=activated,
            slope=slope,
            fetched=forward_fetched,
        )
        output, kept = (output, forward_kept)
        stash.append(kept)
        produced.append(output.astype(jnp.bfloat16))
        if tick < batches:
            received = from_behind(produced[-1], SECTION, 1)
    def pick(earlier, later):
        return earlier if earlier is later else jnp.where(first, earlier, later)

    steps = []
    expert_steps = []
    arriving = jnp.zeros((length, model), jnp.bfloat16)
    results = []
    for tick in range(batches + 1):
        own = data[min(tick, batches - 1)]
        incoming = jnp.where(first, arriving, own).astype(jnp.float32)
        kept = jax.tree.map(pick, stash[max(tick - 1, 0)], stash[min(tick + 1, batches)])
        if tick == 0:
            kept = stash[min(1, batches)]
        elif tick == batches:
            kept = stash[batches - 1]
        grad_out = incoming
        fetched = kept.fetched.astype(jnp.float32)
        gate_grad = jnp.sum(grad_out * fetched, axis=-1)
        weighted = (kept.gate[:, None] * grad_out).astype(jnp.bfloat16)
        outgoing = (
            jnp.dot(kept.place, weighted, preferred_element_type=jnp.float32)
            .astype(jnp.bfloat16)
            .reshape(owners, local * capacity, model)
        )
        arrived_grad = lax.all_to_all(
            outgoing, EXPERT, split_axis=0, concat_axis=0, tiled=True
        ).reshape(owners, local, capacity, model)
        activation_grad = jnp.einsum(
            "secd,edf->secf", arrived_grad, down_w, preferred_element_type=jnp.float32
        )
        before_grad = (activation_grad * kept.slope.astype(jnp.float32)).astype(jnp.bfloat16)
        expert_steps.append(ExpertStep(kept.arrived, kept.activated, arrived_grad, before_grad))
        if tick == batches:
            expert_sums = lax.cond(first, later_sums, empty_sums, *expert_steps[1:])
            kept_sums, before_grad = lax.optimization_barrier((expert_sums, before_grad))
            up_sum, down_sum = kept_sums
            swapped = lax.ppermute(down_sum, SECTION, [(0, 1)])
            late_share = lax.psum_scatter(
                jnp.where(first, up_sum, swapped), DP, scatter_dimension=1, tiled=True
            )
        input_rows_grad = jnp.einsum(
            "secf,edf->secd", before_grad, up_w, preferred_element_type=jnp.float32
        ).astype(jnp.bfloat16)
        back_grad = lax.all_to_all(
            input_rows_grad.reshape(owners, local * capacity, model),
            EXPERT,
            split_axis=0,
            concat_axis=0,
            tiled=True,
        ).reshape(experts * capacity, model)
        routed_grad = jnp.einsum(
            "sl,sd->ld", kept.place, back_grad, preferred_element_type=jnp.float32
        )
        choose = (kept.route[:, None] == expert_ids[None, :]).astype(jnp.float32)
        logit_grad = kept.chances * (
            gate_grad[:, None] * choose - (gate_grad * kept.gate)[:, None]
        )
        routed_full = kept.routed.astype(jnp.float32)
        router_part = jnp.dot(routed_full.T, logit_grad, precision=highest)
        routed_grad = routed_grad + jnp.dot(
            logit_grad, router_w.astype(jnp.float32).T, precision=highest
        )
        second_pull = jax.vjp(normalize, kept.hidden, gain_two)[1]
        hidden_part, gain_two_part = second_pull(routed_grad)
        hidden_grad = grad_out + hidden_part
        branch_grad = hidden_grad.astype(jnp.bfloat16)
        mixed_grad = jnp.einsum(
            "le,ce->lc", branch_grad, output_w, preferred_element_type=jnp.float32
        ).astype(jnp.bfloat16)
        *projected_grad, score_grad = attend_back(
            kept.projected, mixed_grad, relative, kept.segment
        )
        projected_grad = jnp.concatenate(projected_grad, 1)
        normed_grad = jnp.einsum(
            "le,ce->lc", projected_grad, qkv_w, preferred_element_type=jnp.float32
        )
        first_pull = jax.vjp(normalize, kept.inputs.astype(jnp.float32), gain_one)[1]
        input_part, gain_one_part = first_pull(normed_grad)
        steps.append(
            SharedStep(
                kept.normed,
                kept.mixed,
                branch_grad,
                projected_grad,
                router_part,
                gain_one_part,
                gain_two_part,
                score_grad,
            )
        )
        grad_in = hidden_grad + input_part
        results.append(grad_in.astype(jnp.bfloat16))
        if tick < batches:
            arriving = from_behind(results[-1], SECTION, -1)
        if tick == batches - 1:
            up_sum, down_sum = lax.cond(first, empty_sums, later_sums, *expert_steps)
            swapped = lax.ppermute(up_sum, SECTION, [(1, 0)])
            early_share = lax.psum_scatter(
                jnp.where(first, swapped, down_sum), DP, scatter_dimension=1, tiled=True
            )
    blocks = [jnp.where(first, results[index + 1], produced[index + 1]) for index in range(batches)]
    ends_out = jnp.concatenate(blocks, 0)[None]
    parts = merged(steps)
    score_pairs = [part.score_grad for part in parts]
    offsets = offset_sums(score_pairs[0], score_pairs[1])
    table_sum = jnp.dot(bucket_hot, offsets.T, precision=highest)
    projection_sum = jnp.concatenate(
        [
            product([part.normed for part in parts], [part.projected_grad for part in parts]),
            product([part.mixed for part in parts], [part.branch_grad for part in parts]),
        ],
        1,
    ).reshape(layers, owners, piece, 4 * model)
    quarters = lax.all_to_all(projection_sum, EXPERT, split_axis=1, concat_axis=1, tiled=True)
    quarter = quarters.astype(jnp.float32).sum(1).astype(jnp.bfloat16)
    share = lax.psum_scatter(
        quarter.reshape(layers * piece, 4 * model), DP, scatter_dimension=0, tiled=True
    )
    shares = spread(share).reshape(owners * piece, 4 * model).astype(jnp.float32)
    exchanged = lax.ppermute(
        jnp.where(first, early_share, late_share), SECTION, [(0, 1), (1, 0)]
    )
    up_share = jnp.where(first, late_share, exchanged).reshape(experts_up.shape)
    down_share = jnp.where(first, exchanged, early_share).reshape(local, -1, up_w.shape[2])
    small_sum = jnp.concatenate(
        [
            sum(part.gain_one for part in parts).reshape(layers, -1),
            sum(part.gain_two for part in parts).reshape(layers, -1),
            sum(part.router for part in parts).reshape(layers, -1),
            table_sum.reshape(layers, -1),
        ],
        1,
    ).astype(jnp.bfloat16)
    small_share = lax.dynamic_index_in_dim(
        lax.psum(small_sum, (DP, EXPERT)), lax.axis_index(DP), 0, keepdims=False
    ).astype(jnp.float32)
    return (
        ends_out,
        shares[None, :, :model],
        shares[None, :, model : 2 * model],
        shares[None, :, 2 * model : 3 * model],
        shares[None, :, 3 * model :],
        small_share[None, :rows],
        small_share[None, rows : 2 * rows],
        small_share[2 * rows : (2 + kinds) * rows].reshape(1, rows, kinds),
        small_share[(2 + kinds) * rows :].reshape(1, -1, bias_table.shape[2]),
        up_share.astype(jnp.float32),
        jnp.swapaxes(down_share.astype(jnp.float32), 1, 2)[None],
    )


def solution(mesh):
    in_specs = (
        P(SECTION, (DP, EXPERT), None),
        P(SECTION, DP, None),
        P(SECTION, DP, None),
        P(SECTION, DP, None),
        P(SECTION, DP, None),
        P(SECTION, DP),
        P(SECTION, DP),
        P(SECTION, DP, None),
        P(SECTION, DP, None),
        P(SECTION, EXPERT, DP, None),
        P(SECTION, EXPERT, None, DP),
        P(SECTION, (DP, EXPERT)),
        P(SECTION, (DP, EXPERT)),
        P((DP, EXPERT)),
        P(),
    )
    out_specs = (
        P(SECTION, (DP, EXPERT), None),
        P(SECTION, DP, None),
        P(SECTION, DP, None),
        P(SECTION, DP, None),
        P(SECTION, DP, None),
        P(SECTION, DP),
        P(SECTION, DP),
        P(SECTION, DP, None),
        P(SECTION, DP, None),
        P(SECTION, EXPERT, DP, None),
        P(SECTION, EXPERT, None, DP),
    )
    return jax.shard_map(shards, mesh=mesh, in_specs=in_specs, out_specs=out_specs, check_vma=False)
```

time: 1000 us -> 920 us (0.920)
  waiting for transfers between devices: 426 us -> 243 us
  Pallas kernels: 0 us -> 65.2 us
  matrix products: 209 us -> 160 us
  local copies, waits for them, and re-layouts: 148 us -> 183 us
  starting transfers between devices: 57 us -> 77.5 us
  other arithmetic: 45.1 us -> 61 us
  blocking collectives: 87.6 us -> 102 us
    reduce_scatter x3 -> x1, waiting for transfers between devices: 171 us -> 0.02 us  [shards(): lax.psum_scatter(quarter.reshape(layers * piece, 4 * model), DP, scatter_...]
    unnamed x362 -> x211, local copies, waits for them, and re-layouts: 38.9 us -> 126 us
    pallas_call x0 -> x8, Pallas kernels: none -> 65.2 us  [the longest x3 27.9 us: attend_back(): pl.pallas_call(functools.partial(backward_body, model // heads), grid=(gr...]
    all_gather x3 -> x2, waiting for transfers between devices: 178 us -> 129 us  [the longest x1 65.7 us: shards(): lax.all_gather(jnp.where(first, own_up, swapped), DP, axis=1, tiled=True)]
    dot_general x41 -> x18, matrix products: 119 us -> 77.9 us  [the longest x3 24.9 us: shards(): jnp.einsum('secd,edf->secf', arrived, tick_up, preferred_element_type=jnp...]
    rev x2 -> x1, local copies, waits for them, and re-layouts: 41.2 us -> 0.1 us  [shards(): buckets[:length][::-1]]
    another operation x2 -> x8, local copies, waits for them, and re-layouts: 0.3 us -> 24.4 us
    select_n x0 -> x7, other arithmetic: none -> 22.3 us  [the longest x1 5.1 us: shards(): up_w = jnp.where(first, early_w, late_up)]
  transfers between devices with their start and end apart: 23 -> 30, of which waited for: 17 -> 18; matrix products, arithmetic and copies ran while one was open for 22% -> 27% of each run, Pallas kernels for 0% -> 3%
where the time goes in v1:
time: 920 us; the launch traced here: 909 us
  waiting for transfers between devices  243 us (26%)
  local copies, waits for them, and re-layouts  183 us (20%)
  matrix products  160 us (17%)
  blocking collectives  102 us (11%)
  starting transfers between devices  77.5 us (8%)
  Pallas kernels  65.2 us (7%)
  other arithmetic  61 us (7%)
  between operations  15.9 us (2%)
    unnamed x211, local copies, waits for them, and re-layouts  126 us
    psum x1, blocking collectives, shards(): lax.psum(small_sum, (DP, EXPERT))  76.2 us
    all_gather x1, waiting for transfers between devices, shards(): lax.all_gather(jnp.where(first, own_up, swapped), DP, axis=1, tiled=True)  65.7 us
    all_gather x1, waiting for transfers between devices, shards(): lax.all_gather(jnp.where(first, swapped, own_down), DP, axis=1, tiled=True)  63.4 us
    all_gather x1, waiting for transfers between devices, shards(): lax.all_gather(lax.dynamic_slice_in_dim(projections, mine * piece, piece,...  29.3 us
    pallas_call x3, Pallas kernels, attend_back(): pl.pallas_call(functools.partial(backward_body, model // heads), grid=(gr...  27.9 us
    dot_general x3, matrix products, shards(): jnp.einsum('secd,edf->secf', arrived, tick_up, preferred_element_type=jnp...  24.9 us
    another operation x8, local copies, waits for them, and re-layouts  24.4 us
  transfers between devices with their start and end apart: 30, of which 18 were waited for; matrix products, arithmetic and copies ran while one was open for 27% of the time, Pallas kernels for 3%

profile of v1, /device:TPU:0, one launch (start us, length us, event | category | flops | bytes accessed | tf_op | source)
XLA Modules:
  0.0 908.7 jit_solution(14472128206396299913)
XLA Ops:
  14.1 29.3 %all-gather.10.cloned.1.call-done = bf16[192,3072]{1,0:T(8,128)(2,1)} async-done(((bf16[48,3072]{1,0:T(8,128)(2,1)}), bf16[192,3072]{1,0:T(8,128)(2,1)}) %all-gather.10.cloned.1.call-update) | async-done | bytes 1179664 | tf_op jit(solution)/shard_map/all_gather | solution.py:251
  50.3 5.2 all-to-all-start
  56.1 13.4 %all-gather.1 = bf16[4,1,1248]{2,1,0:T(2,128)(2,1)S(1)} all-gather(bf16[1,1,1248]{2,1,0:T(2,128)(2,1)S(1)} %bitcast.477), channel_id=1, replica_groups=mesh['section'=2,'dp'=4,'expert'=4] {'dp'}, dimensions={0}, use_global_device_ids=true | all-gather | bytes 12480 | tf_op jit(solution)/shard_map/all_gather | solution.py:264
  69.5 65.7 %all-gather.6.cloned.1.call-done = bf16[1,768,3072]{2,1,0:T(8,128)(2,1)} async-done(((bf16[1,192,3072]{2,1,0:T(8,128)(2,1)}), bf16[1,768,3072]{2,1,0:T(8,128)(2,1)}) %all-gather.6.cloned.1.call-update) | async-done | bytes 4718608 | tf_op jit(solution)/shard_map/all_gather | solution.py:277
  138.2 7.1 spread_offsets.1.bias
  153.5 7.0 attend.3
  162.0 63.4 %all-gather.8.cloned.1.call-done = bf16[1,768,3072]{2,1,0:T(8,128)(2,1)} async-done(((bf16[1,192,3072]{2,1,0:T(8,128)(2,1)}), bf16[1,768,3072]{2,1,0:T(8,128)(2,1)}) %all-gather.8.cloned.1.call-update) | async-done | bytes 4718608 | tf_op jit(solution)/shard_map/all_gather | solution.py:278
  232.6 4.2 all-to-all-start.1
  238.1 7.2 all-to-all-done.1
  245.4 8.3 fusion.62
  255.3 5.8 fusion.165
  261.1 4.7 all-to-all-start.2
  265.8 5.0 broadcast_select_fusion.2
  280.3 5.1 broadcast_select_fusion.3
  287.0 7.0 attend.4
  304.5 5.7 all-to-all-done.4
  310.1 4.2 all-to-all-start.3
  314.3 8.3 fusion.67
  324.3 5.8 fusion.160
  330.2 4.4 all-to-all-start.6
  334.5 6.0 fusion.56
  342.2 5.8 fusion.180
  348.0 4.2 all-to-all-start.5
  372.6 4.4 broadcast_select_fusion.7
  377.0 7.0 attend.5
  385.5 9.3 %attend_back.3 = (bf16[256,768]{1,0:T(8,128)(2,1)S(1)}, bf16[256,768]{1,0:T(8,128)(2,1)S(1)}, bf16[256,768]{1,0:T(8,128)(2,1)S(1)}, bf16[12,256,256]{2,1,0:T(8,128)(2,1)S(1)}) custom-call(s32[256,1]{1,0:T(8,128)S(1)} %copy.108.column, s32[1,256]{1,0:T(1,128)S(1)} %bitcast.402, bf16[256,2304]{1,0:T(8,128)(2,1)S(1)} %copy-done.2, ...), custom_call_target="tpu_custom_call" | custom-call | tf_op jit(solution)/shard_map/attend_back/pallas_call | solution.py:179
  401.3 4.4 all-to-all-start.8
  409.4 5.0 fusion.193
  417.5 8.3 fusion.72
  427.5 5.8 fusion.155
  433.3 4.2 all-to-all-start.10
  442.7 5.9 all-to-all-done.10
  455.5 12.9 %all_to_all.75 = bf16[4,128,768]{2,1,0:T(8,128)(2,1)S(1)} all-to-all(bf16[4,128,768]{2,1,0:T(8,128)(2,1)S(1)} %bitcast.462), channel_id=1, replica_groups=mesh['section'=2,'dp'=4,'expert'=4] {'expert'}, dimensions={0} | all-to-all | bytes 1572864 | tf_op jit(solution)/shard_map/all_to_all | solution.py:441
  468.3 6.0 fusion.73
  479.5 4.6 all-to-all-start.9
  484.2 8.3 all-to-all-done.9
  502.1 9.3 %attend_back.4 = (bf16[256,768]{1,0:T(8,128)(2,1)S(1)}, bf16[256,768]{1,0:T(8,128)(2,1)S(1)}, bf16[256,768]{1,0:T(8,128)(2,1)S(1)}, bf16[12,256,256]{2,1,0:T(8,128)(2,1)S(1)}) custom-call(s32[256,1]{1,0:T(8,128)S(1)} %copy.123.column, s32[1,256]{1,0:T(1,128)S(1)} %bitcast.405, bf16[256,2304]{1,0:T(8,128)(2,1)S(1)} %copy-done.6, ...), custom_call_target="tpu_custom_call" | custom-call | tf_op jit(solution)/shard_map/attend_back/pallas_call | solution.py:179
  522.1 4.2 all-to-all-start.11
  532.3 5.3 all-to-all-done.11
  537.6 7.1 fusion.57
  544.8 37.0 %conditional.2 = (bf16[1,768,3072]{2,1,0:T(8,128)(2,1)}, bf16[1,768,3072]{2,1,0:T(8,128)(2,1)}) conditional(s32[]{:T(128)} %convert_element_type.390, () %tuple.33, (bf16[4,1,128,768]{3,2,0,1:T(8,128)(2,1)}, bf16[4,128,768]{2,1,0:T(8,128)(2,1)}, bf16[4,1,128,3072]{2,3,0,1:T(8,128)(2,1)}, bf16[4,1,128,3072]{2,3,0,1:T(8,128)(2,1)}, ...), branch_computations={%region_23.24_spmd, %region_24.25_spmd} | conditional | flops 9699852288 | bytes 50331664 | solution.py:450
  544.9 4.7 copy.127
  549.6 4.7 copy.126
  554.3 9.1 %fusion.14 = bf16[1,768,3072]{2,1,0:T(8,128)(2,1)} fusion(bf16[512,3072]{1,0:T(8,128)(2,1)} %bitcast.439, bf16[512,3072]{1,0:T(8,128)(2,1)} %bitcast.440, bf16[512,768]{1,0:T(8,128)(2,1)} %bitcast.2, bf16[512,768]{1,0:T(8,128)(2,1)} %bitcast.454), kind=kOutput, calls=%fused_computation.10 | convolution fusion | flops 4849926144 | bytes 12582912 | tf_op jit(solution)/shard_map/cond/branch_1_fun/dot_general | solution.py:311
  563.4 4.7 copy.129
  568.0 4.6 copy.128
  572.7 9.1 %fusion.17 = bf16[1,768,3072]{2,1,0:T(8,128)(2,1)} fusion(bf16[512,3072]{1,0:T(8,128)(2,1)} %bitcast.441, bf16[512,3072]{1,0:T(8,128)(2,1)} %bitcast.442, bf16[512,768]{1,0:T(8,128)(2,1)} %bitcast.7, bf16[512,768]{1,0:T(8,128)(2,1)} %bitcast.456), kind=kOutput, calls=%fused_computation.11 | convolution fusion | flops 4849926144 | bytes 12582912 | tf_op jit(solution)/shard_map/cond/branch_1_fun/dot_general | solution.py:311
  581.8 6.8 fusion.170
  588.6 4.4 all-to-all-start.12
  597.2 4.7 all-to-all-done.12
  609.0 9.3 %attend_back.5 = (bf16[256,768]{1,0:T(8,128)(2,1)S(1)}, bf16[256,768]{1,0:T(8,128)(2,1)S(1)}, bf16[256,768]{1,0:T(8,128)(2,1)S(1)}, bf16[12,256,256]{2,1,0:T(8,128)(2,1)S(1)}) custom-call(s32[256,1]{1,0:T(8,128)S(1)} %copy.108.column, s32[1,256]{1,0:T(1,128)S(1)} %bitcast.403, bf16[256,2304]{1,0:T(8,128)(2,1)S(1)} %copy-done.3, ...), custom_call_target="tpu_custom_call" | custom-call | tf_op jit(solution)/shard_map/attend_back/pallas_call | solution.py:179
  626.6 5.2 all-to-all-start.13
  631.8 5.8 conditional.3
  639.0 22.0 %all-to-all-done.13 = bf16[4,4,48,3072]{3,2,0,1:T(8,128)(2,1)} async-done(((bf16[4,4,48,3072]{3,2,0,1:T(8,128)(2,1)}), bf16[4,4,48,3072]{3,2,0,1:T(8,128)(2,1)}, u32[]{:S(2)}, u32[]{:S(2)}) %all-to-all-start.13) | async-done | bytes 4718624 | tf_op jit(solution)/shard_map/all_to_all | solution.py:530
  660.9 4.6 reduce_sum.308
  668.4 42.6 %copy.190 = bf16[1,768,3072]{2,0,1:T(2,128)(2,1)S(1)} copy(bf16[1,768,3072]{2,1,0:T(8,128)(2,1)S(1)} %broadcast_select_fusion) | data formatting | bytes 9437184
  716.8 7.3 collective-permute-done.7
  727.1 42.6 %copy.191 = bf16[1,768,3072]{2,0,1:T(2,128)(2,1)S(1)} copy(bf16[1,768,3072]{2,1,0:T(8,128)(2,1)S(1)} %broadcast_select_fusion.1) | data formatting | bytes 9437184
  776.1 4.6 fusion.192
  782.2 9.2 %offset_sums.1 = f32[12,1,512]{2,1,0:T(1,128)} custom-call(bf16[12,256,256]{2,1,0:T(8,128)(2,1)} %copy-done.11, bf16[12,256,256]{2,1,0:T(8,128)(2,1)} %broadcast_select_fusion.5.two), custom_call_target="tpu_custom_call" | custom-call | tf_op jit(solution)/shard_map/offset_sums/pallas_call | solution.py:205
  792.6 76.2 %psum.7 = bf16[4,1248]{1,0:T(4,128)(2,1)S(1)} all-reduce(bf16[4,1248]{1,0:T(4,128)(2,1)S(1)} %concatenate.76), channel_id=1, replica_groups=mesh['section'=2,'dp'=4,'expert'=4] {'dp','expert'}, use_global_device_ids=true, to_apply=%region_36.37 | all-reduce | flops 4992 | bytes 19968 | tf_op jit(solution)/shard_map/psum | solution.py:551
  874.6 4.3 all-to-all-start.14
  881.4 5.3 reduce-scatter.10.cloned.1.call-done
  897.3 4.3 convert_bitcast_fusion
  (393 shorter events, 207.3 us)
Async XLA Ops:
  7.2 36.2 %copy-start.42 = (bf16[1,1,192,3072]{3,2,1,0:T(8,128)(2,1)S(1)}, bf16[1,1,192,3072]{3,2,1,0:T(8,128)(2,1)}, u32[]{:S(2)}) copy-start(bf16[1,1,192,3072]{3,2,1,0:T(8,128)(2,1)} %param.28) | copy-start | bytes 3538948
  7.2 36.2 %copy-start.41 = (bf16[1,1,3072,192]{2,3,1,0:T(8,128)(2,1)S(1)}, bf16[1,1,3072,192]{2,3,1,0:T(8,128)(2,1)}, u32[]{:S(2)}) copy-start(bf16[1,1,3072,192]{2,3,1,0:T(8,128)(2,1)} %param.29) | copy-start | bytes 3538948
  7.2 36.2 %all-gather.10.cloned.1.call-start = ((), (), s32[]{:S(2)}) async-start(), calls=%async_computation.21 | async-start | bytes 1474560 | tf_op jit(solution)/shard_map/all_gather | solution.py:251
  9.2 126.0 %all-gather.6.cloned.1.call-start = ((), (), s32[]{:S(2)}) async-start(), calls=%async_computation.18 | async-start | bytes 5898240 | tf_op jit(solution)/shard_map/all_gather | solution.py:277
  11.0 3.1 collective-permute-start
  46.3 179.1 %all-gather.8.cloned.1.call-start = ((), (), s32[]{:S(2)}) async-start(), calls=%async_computation.19 | async-start | bytes 5898240 | tf_op jit(solution)/shard_map/all_gather | solution.py:278
  50.3 86.3 %copy-start.85 = (s32[512]{0:T(512)S(1)}, s32[512]{0:T(512)}, u32[]{:S(2)}) copy-start(s32[512]{0:T(512)} %param.32) | copy-start | bytes 6148
  50.3 86.9 %slice-start.8 = ((s32[511]{0:T(512)}), s32[256]{0:T(256)S(1)}, s32[]{:S(2)}) async-start(s32[511]{0:T(512)} %param.33), calls=%async_computation.32 | async-start | bytes 2048 | tf_op jit(solution)/shard_map/slice | solution.py:294
  50.3 96.3 %all-to-all-start = ((bf16[4,4,48,3072]{3,2,1,0:T(8,128)(2,1)}), bf16[4,4,48,3072]{3,2,1,0:T(8,128)(2,1)}, u32[]{:S(2)}, u32[]{:S(2)}) async-start(bf16[4,4,48,3072]{3,2,1,0:T(8,128)(2,1)} %broadcast_in_dim.51), calls=%async_computation | async-start | bytes 9437184 | tf_op jit(solution)/shard_map/all_to_all | solution.py:256
  55.6 90.9 %copy-start.30 = (bf16[1,512,768]{2,1,0:T(8,128)(2,1)S(1)}, bf16[1,512,768]{2,1,0:T(8,128)(2,1)}, u32[]{:S(2)}) copy-start(bf16[1,512,768]{2,1,0:T(8,128)(2,1)} %param.19) | copy-start | bytes 2359300
  55.6 91.1 %copy-start.82 = (s32[1,512]{1,0:T(1,128)S(1)}, s32[1,512]{1,0:T(1,128)}, u32[]{:S(2)}) copy-start(s32[1,512]{1,0:T(1,128)} %param.31) | copy-start | bytes 6148
  55.6 91.1 %copy-start.83 = (s32[1,512]{1,0:T(1,128)S(1)}, s32[1,512]{1,0:T(1,128)}, u32[]{:S(2)}) copy-start(s32[1,512]{1,0:T(1,128)} %param.30) | copy-start | bytes 6148
  135.2 118.5 %collective-permute-start.2 = (bf16[1,768,3072]{2,1,0:T(8,128)(2,1)}, bf16[1,768,3072]{2,1,0:T(8,128)(2,1)}, u32[]{:S(2)}, u32[]{:S(2)}) collective-permute-start(bf16[1,768,3072]{2,1,0:T(8,128)(2,1)} %all-gather.6.cloned.1.call-done), channel_id=1, source_target_pairs={{16,0},{17,1},{18,2},{19,3},{20,4},{21,5},{22,6},{23,7},{24,8},{25... | collective-permute-start | bytes 14155784 | tf_op jit(solution)/shard_map/ppermute | solution.py:279
  149.5 11.0 %copy-start.27 = (bf16[4,4,48,3072]{3,2,0,1:T(8,128)(2,1)}, bf16[4,4,48,3072]{3,2,0,1:T(8,128)(2,1)S(1)}, u32[]{:S(2)}) copy-start(bf16[4,4,48,3072]{3,2,0,1:T(8,128)(2,1)S(1)} %copy.103) | copy-start | bytes 14155780
  150.7 9.9 %copy-start.4 = (bf16[256,2304]{1,0:T(8,128)(2,1)}, bf16[256,2304]{1,0:T(8,128)(2,1)S(1)}, u32[]{:S(2)}) copy-start(bf16[256,2304]{1,0:T(8,128)(2,1)S(1)} %convolution_convert_fusion.3.query.key.value) | copy-start | bytes 3538948
  225.3 55.0 %collective-permute-start.1 = (bf16[1,768,3072]{2,1,0:T(8,128)(2,1)}, bf16[1,768,3072]{2,1,0:T(8,128)(2,1)}, u32[]{:S(2)}, u32[]{:S(2)}) collective-permute-start(bf16[1,768,3072]{2,1,0:T(8,128)(2,1)} %all-gather.8.cloned.1.call-done), channel_id=1, source_target_pairs={{0,16},{1,17},{2,18},{3,19},{4,20},{5,21},{6,22},{7,23},{8,24},{9,... | collective-permute-start | bytes 14155784 | tf_op jit(solution)/shard_map/ppermute | solution.py:280
  232.6 12.8 %all-to-all-start.1 = ((bf16[4,128,768]{2,1,0:T(8,128)(2,1)}), bf16[4,128,768]{2,1,0:T(8,128)(2,1)}, u32[]{:S(2)}, u32[]{:S(2)}) async-start(bf16[4,128,768]{2,1,0:T(8,128)(2,1)} %bitcast.449), calls=%async_computation.1 | async-start | bytes 1572864 | tf_op jit(solution)/shard_map/all_to_all | solution.py:374
  261.1 12.8 %all-to-all-start.2 = ((bf16[4,128,768]{1,2,0:T(8,128)(2,1)}), bf16[4,128,768]{1,2,0:T(8,128)(2,1)}, u32[]{:S(2)}, u32[]{:S(2)}) async-start(bf16[4,128,768]{1,2,0:T(8,128)(2,1)} %fusion.165), calls=%async_computation.2 | async-start | bytes 1572864 | tf_op jit(solution)/shard_map/all_to_all | solution.py:384
  278.7 7.1 slice-start
  278.7 7.1 slice-start.1
  278.7 6.7 collective-permute-start.3
  285.6 8.4 copy-start.39
  297.9 12.3 %all-to-all-start.4 = ((bf16[4,128,768]{2,1,0:T(8,128)(2,1)}), bf16[4,128,768]{2,1,0:T(8,128)(2,1)}, u32[]{:S(2)}, u32[]{:S(2)}) async-start(bf16[4,128,768]{2,1,0:T(8,128)(2,1)} %bitcast.450), calls=%async_computation.4 | async-start | bytes 1572864 | tf_op jit(solution)/shard_map/all_to_all | solution.py:374
  310.1 20.0 %all-to-all-start.3 = ((bf16[4,128,768]{2,1,0:T(8,128)(2,1)}), bf16[4,128,768]{2,1,0:T(8,128)(2,1)}, u32[]{:S(2)}, u32[]{:S(2)}) async-start(bf16[4,128,768]{2,1,0:T(8,128)(2,1)} %bitcast.458), calls=%async_computation.3 | async-start | bytes 1572864 | tf_op jit(solution)/shard_map/all_to_all | solution.py:441
  330.2 17.9 %all-to-all-start.6 = ((bf16[4,128,768]{1,2,0:T(8,128)(2,1)}), bf16[4,128,768]{1,2,0:T(8,128)(2,1)}, u32[]{:S(2)}, u32[]{:S(2)}) async-start(bf16[4,128,768]{1,2,0:T(8,128)(2,1)} %fusion.160), calls=%async_computation.6 | async-start | bytes 1572864 | tf_op jit(solution)/shard_map/all_to_all | solution.py:384
  348.0 12.3 %all-to-all-start.5 = ((bf16[4,128,768]{1,2,0:T(8,128)(2,1)}), bf16[4,128,768]{1,2,0:T(8,128)(2,1)}, u32[]{:S(2)}, u32[]{:S(2)}) async-start(bf16[4,128,768]{1,2,0:T(8,128)(2,1)} %fusion.180), calls=%async_computation.5 | async-start | bytes 1572864 | tf_op jit(solution)/shard_map/all_to_all | solution.py:460
  357.1 9.5 %copy-start.73 = (f32[256]{0:T(256)}, f32[256]{0:T(256)S(1)}, u32[]{:S(2)}) copy-start(f32[256]{0:T(256)S(1)} %get-tuple-element.276) | copy-start | bytes 3076
  366.6 3.0 collective-permute-start.5
  369.6 14.4 %slice-start.2 = ((s8[4718592]{0:T(1024)(128)(4,1)}), s8[4194304]{0:T(1024)(128)(4,1)S(1)}, s32[]{:S(2)}) async-start(s8[4718592]{0:T(1024)(128)(4,1)} %bitcast.426), calls=%async_computation.26 | async-start | bytes 8388608
  372.4 11.6 %copy-start.43 = (bf16[256,768]{1,0:T(8,128)(2,1)}, bf16[256,768]{1,0:T(8,128)(2,1)S(1)}, u32[]{:S(2)}) copy-start(bf16[256,768]{1,0:T(8,128)(2,1)S(1)} %get-tuple-element.218) | copy-start | bytes 1179652
  372.4 12.4 %copy-start.25 = (f32[256,768]{1,0:T(8,128)}, f32[256,768]{1,0:T(8,128)S(1)}, u32[]{:S(2)}) copy-start(f32[256,768]{1,0:T(8,128)S(1)} %get-tuple-element.248) | copy-start | bytes 2359300
  372.6 11.5 %slice-start.3 = ((s8[4718592]{0:T(1024)(128)(4,1)}), s8[524288]{0:T(1024)(128)(4,1)S(1)}, s32[]{:S(2)}) async-start(s8[4718592]{0:T(1024)(128)(4,1)} %bitcast.426), calls=%async_computation.27 | async-start | bytes 1048576
  384.9 13.4 %copy-start.55 = (f32[256,768]{1,0:T(8,128)}, f32[256,768]{1,0:T(8,128)S(1)}, u32[]{:S(2)}) copy-start(f32[256,768]{1,0:T(8,128)S(1)} %get-tuple-element.280) | copy-start | bytes 2359300
  385.5 12.8 %copy-start.37 = (f32[256,768]{1,0:T(8,128)S(1)}, f32[256,768]{1,0:T(8,128)}, u32[]{:S(2)}) copy-start(f32[256,768]{1,0:T(8,128)} %get-tuple-element.267) | copy-start | bytes 2359300
  401.3 16.2 %all-to-all-start.8 = ((bf16[4,128,768]{2,1,0:T(8,128)(2,1)}), bf16[4,128,768]{2,1,0:T(8,128)(2,1)}, u32[]{:S(2)}, u32[]{:S(2)}) async-start(bf16[4,128,768]{2,1,0:T(8,128)(2,1)} %bitcast.448), calls=%async_computation.8 | async-start | bytes 1572864 | tf_op jit(solution)/shard_map/all_to_all | solution.py:374
  433.3 15.2 %all-to-all-start.10 = ((bf16[4,128,768]{1,2,0:T(8,128)(2,1)}), bf16[4,128,768]{1,2,0:T(8,128)(2,1)}, u32[]{:S(2)}, u32[]{:S(2)}) async-start(bf16[4,128,768]{1,2,0:T(8,128)(2,1)} %fusion.155), calls=%async_computation.10 | async-start | bytes 1572864 | tf_op jit(solution)/shard_map/all_to_all | solution.py:384
  440.0 10.8 %collective-permute-start.4 = (bf16[256,768]{1,0:T(8,128)(2,1)}, bf16[256,768]{1,0:T(8,128)(2,1)}, u32[]{:S(2)}, u32[]{:S(2)}) collective-permute-start(bf16[256,768]{1,0:T(8,128)(2,1)} %fusion.198), channel_id=1, source_target_pairs={{16,0},{17,1},{18,2},{19,3},{20,4},{21,5},{22,6},{23,7},{24,8},{25... | collective-permute-start | bytes 1179656 | tf_op jit(solution)/shard_map/ppermute | solution.py:55
  450.8 17.5 %copy-start.88 = (bf16[4,1,128,3072]{2,3,0,1:T(8,128)(2,1)S(1)}, bf16[4,1,128,3072]{2,3,0,1:T(8,128)(2,1)}, u32[]{:S(2)}) copy-start(bf16[4,1,128,3072]{2,3,0,1:T(8,128)(2,1)} %get-tuple-element.98) | copy-start | bytes 9437188
  450.8 17.5 %copy-start.89 = (bf16[4,1,128,3072]{2,3,0,1:T(8,128)(2,1)S(1)}, bf16[4,1,128,3072]{2,3,0,1:T(8,128)(2,1)}, u32[]{:S(2)}) copy-start(bf16[4,1,128,3072]{2,3,0,1:T(8,128)(2,1)} %get-tuple-element.99) | copy-start | bytes 9437188
  453.7 22.3 %slice-start.6 = ((s8[4718592]{0:T(1024)(128)(4,1)}), s8[4194304]{0:T(1024)(128)(4,1)S(1)}, s32[]{:S(2)}) async-start(s8[4718592]{0:T(1024)(128)(4,1)} %bitcast.434), calls=%async_computation.30 | async-start | bytes 8388608
  468.3 7.6 slice-start.7
  479.5 13.0 %all-to-all-start.9 = ((bf16[4,128,768]{1,2,0:T(8,128)(2,1)}), bf16[4,128,768]{1,2,0:T(8,128)(2,1)}, u32[]{:S(2)}, u32[]{:S(2)}) async-start(bf16[4,128,768]{1,2,0:T(8,128)(2,1)} %fusion.175), calls=%async_computation.9 | async-start | bytes 1572864 | tf_op jit(solution)/shard_map/all_to_all | solution.py:460
  498.5 13.1 %slice-start.4 = ((s8[4718592]{0:T(1024)(128)(4,1)}), s8[4194304]{0:T(1024)(128)(4,1)S(1)}, s32[]{:S(2)}) async-start(s8[4718592]{0:T(1024)(128)(4,1)} %bitcast.430), calls=%async_computation.28 | async-start | bytes 8388608
  502.1 9.5 %slice-start.5 = ((s8[4718592]{0:T(1024)(128)(4,1)}), s8[524288]{0:T(1024)(128)(4,1)S(1)}, s32[]{:S(2)}) async-start(s8[4718592]{0:T(1024)(128)(4,1)} %bitcast.430), calls=%async_computation.29 | async-start | bytes 1048576
  502.1 9.5 %copy-start.59 = (bf16[256,768]{1,0:T(8,128)(2,1)S(1)}, bf16[256,768]{1,0:T(8,128)(2,1)}, u32[]{:S(2)}) copy-start(bf16[256,768]{1,0:T(8,128)(2,1)} %get-tuple-element.217) | copy-start | bytes 1179652
  514.5 3.9 collective-permute-start.6
  522.1 15.6 %all-to-all-start.11 = ((bf16[4,128,768]{2,1,0:T(8,128)(2,1)}), bf16[4,128,768]{2,1,0:T(8,128)(2,1)}, u32[]{:S(2)}, u32[]{:S(2)}) async-start(bf16[4,128,768]{2,1,0:T(8,128)(2,1)} %bitcast.447), calls=%async_computation.11 | async-start | bytes 1572864 | tf_op jit(solution)/shard_map/all_to_all | solution.py:441
  588.6 13.3 %all-to-all-start.12 = ((bf16[4,128,768]{1,2,0:T(8,128)(2,1)}), bf16[4,128,768]{1,2,0:T(8,128)(2,1)}, u32[]{:S(2)}, u32[]{:S(2)}) async-start(bf16[4,128,768]{1,2,0:T(8,128)(2,1)} %fusion.170), calls=%async_computation.12 | async-start | bytes 1572864 | tf_op jit(solution)/shard_map/all_to_all | solution.py:460
  606.9 11.5 %copy-start.35 = (f32[256,768]{1,0:T(8,128)}, f32[256,768]{1,0:T(8,128)S(1)}, u32[]{:S(2)}) copy-start(f32[256,768]{1,0:T(8,128)S(1)} %get-tuple-element.211) | copy-start | bytes 2359300
  609.0 9.5 %copy-start.57 = (bf16[256,2304]{1,0:T(8,128)(2,1)S(1)}, bf16[256,2304]{1,0:T(8,128)(2,1)}, u32[]{:S(2)}) copy-start(bf16[256,2304]{1,0:T(8,128)(2,1)} %constant_dynamic-update-slice_fusion) | copy-start | bytes 3538948
  626.6 34.4 %all-to-all-start.13 = ((bf16[4,4,48,3072]{3,2,0,1:T(8,128)(2,1)}), bf16[4,4,48,3072]{3,2,0,1:T(8,128)(2,1)}, u32[]{:S(2)}, u32[]{:S(2)}) async-start(bf16[4,4,48,3072]{3,2,0,1:T(8,128)(2,1)} %copy.134), calls=%async_computation.13 | async-start | bytes 9437184 | tf_op jit(solution)/shard_map/all_to_all | solution.py:530
  631.8 240.7 %reduce-scatter.8.cloned.1.call-start = ((), (), s32[]{:S(2)}) async-start(), calls=%async_computation.20 | async-start | bytes 1474560 | tf_op jit(solution)/shard_map/reduce_scatter | solution.py:532
  637.7 27.9 %collective-permute-start.8 = (bf16[1,768,3072]{2,1,0:T(8,128)(2,1)}, bf16[1,768,3072]{2,1,0:T(8,128)(2,1)}, u32[]{:S(2)}, u32[]{:S(2)}) collective-permute-start(bf16[1,768,3072]{2,1,0:T(8,128)(2,1)} %get-tuple-element.115), channel_id=1, source_target_pairs={{16,0},{17,1},{18,2},{19,3},{20,4},{21,5},{22,6},{23,7},{24,8},{25... | collective-permute-start | bytes 14155784 | tf_op jit(solution)/shard_map/ppermute | solution.py:513
  665.5 213.4 %reduce-scatter.12.cloned.1.call-start = ((), (), s32[]{:S(2)}) async-start(), calls=%async_computation.23 | async-start | bytes 5898240
  715.0 171.7 %reduce-scatter.10.cloned.1.call-start = ((), (), s32[]{:S(2)}) async-start(), calls=%async_computation.22 | async-start | bytes 5898240
  715.1 9.0 collective-permute-start.7
  780.9 10.5 %copy-start.78 = (s32[511]{0:T(512)S(1)}, s32[511]{0:T(512)}, u32[]{:S(2)}) copy-start(s32[511]{0:T(512)} %param.33) | copy-start | bytes 6136
  780.9 90.2 %copy-start.80 = (f32[256]{0:T(256)S(1)}, f32[256]{0:T(256)}, u32[]{:S(2)}) copy-start(f32[256]{0:T(256)} %get-tuple-element.226) | copy-start | bytes 3076
  782.2 88.8 %copy-start.36 = (f32[256,768]{1,0:T(8,128)S(1)}, f32[256,768]{1,0:T(8,128)}, u32[]{:S(2)}) copy-start(f32[256,768]{1,0:T(8,128)} %copy-done.35) | copy-start | bytes 2359300
  782.2 88.8 %copy-start.40 = (bf16[256,768]{1,0:T(8,128)(2,1)S(1)}, bf16[256,768]{1,0:T(8,128)(2,1)}, u32[]{:S(2)}) copy-start(bf16[256,768]{1,0:T(8,128)(2,1)} %copy-done.39) | copy-start | bytes 1179652
  782.2 88.9 %copy-start.56 = (f32[256,768]{1,0:T(8,128)S(1)}, f32[256,768]{1,0:T(8,128)}, u32[]{:S(2)}) copy-start(f32[256,768]{1,0:T(8,128)} %copy-done.55) | copy-start | bytes 2359300
  782.2 88.9 %copy-start.63 = (f32[256,768]{1,0:T(8,128)S(1)}, f32[256,768]{1,0:T(8,128)}, u32[]{:S(2)}) copy-start(f32[256,768]{1,0:T(8,128)} %get-tuple-element.291) | copy-start | bytes 2359300
  874.6 18.7 %all-to-all-start.14 = ((bf16[4,48,3072]{2,1,0:T(8,128)(2,1)}), bf16[4,48,3072]{2,1,0:T(8,128)(2,1)}, u32[]{:S(2)}, u32[]{:S(2)}) async-start(bf16[4,48,3072]{2,1,0:T(8,128)(2,1)} %broadcast_in_dim.66), calls=%async_computation.15 | async-start | bytes 2359296 | tf_op jit(solution)/shard_map/all_to_all | solution.py:256
  892.4 3.9 collective-permute-start.9
  (64 other events, 164.3 us)
Sparse Core Ops, SparseCore 0:
  10.2 33.1 all-gather.9
  46.4 88.7 all-gather.5
  137.3 87.9 all-gather.7
  665.6 26.6 reduce-scatter.7
  715.1 82.7 reduce-scatter.11
  800.1 86.5 reduce-scatter.9

commit v2 on v1

--- a/solution.py
+++ b/solution.py
@@ -270,20 +270,14 @@
     table = small[:, (2 + kinds) * rows :].reshape(-1, bias_table.shape[2]).astype(jnp.float32)
     own_up = experts_up[0]
     own_down = jnp.swapaxes(experts_down[0], 1, 2)
-    swapped = lax.ppermute(jnp.where(first, own_down, own_up), SECTION, [(0, 1), (1, 0)])
-    own_up, own_down, swapped, quarter = lax.optimization_barrier(
-        (own_up, own_down, swapped, quarter)
-    )
+    swapped = lax.ppermute(own_down, SECTION, [(0, 1), (1, 0)])
+    own_up, swapped, quarter = lax.optimization_barrier((own_up, swapped, quarter))
     early_w = lax.all_gather(jnp.where(first, own_up, swapped), DP, axis=1, tiled=True)
-    late_w = lax.all_gather(jnp.where(first, swapped, own_down), DP, axis=1, tiled=True)
-    early_down = lax.ppermute(early_w, SECTION, [(1, 0)])
-    late_up = lax.ppermute(late_w, SECTION, [(0, 1)])
-    up_w = jnp.where(first, early_w, late_up)
-    down_w = jnp.where(first, early_down, late_w)
+    late_w = lax.all_gather(jnp.where(first, swapped, own_up), DP, axis=1, tiled=True)
     gathered = jnp.swapaxes(spread(quarter), 0, 1).reshape(layers * owners * piece, -1)
     qkv_w = gathered[:, : 3 * model]
     output_w = gathered[:, 3 * model :]
-    local = up_w.shape[0]
+    local = own_up.shape[0]
     experts = owners * local
     capacity = 2 * length // experts
     heads = table.shape[1]
@@ -308,12 +302,17 @@
         return all_steps[1:batches] + [ends_step]
 
     def product(lefts, rights):
-        return lax.dot_general(
-            jnp.concatenate(lefts, 0),
-            jnp.concatenate(rights, 0),
-            (((0,), (0,)), ((), ())),
-            preferred_element_type=jnp.float32,
+        return sum(
+            lax.dot_general(
+                left, right, (((0,), (0,)), ((), ())), preferred_element_type=jnp.float32
+            )
+            for left, right in zip(lefts, rights)
         ).astype(jnp.bfloat16)
+
+    def scatter(values):
+        if local == 1:
+            return lax.psum_scatter(values[0], DP, scatter_dimension=0, tiled=True)[None]
+        return lax.psum_scatter(values, DP, scatter_dimension=1, tiled=True)
 
     def expert_product(lefts, rights):
         return jnp.stack(
@@ -337,7 +336,7 @@
         )
 
     def empty_sums(*all_steps):
-        shape = up_w.shape
+        shape = early_w.shape
         return jnp.zeros(shape, jnp.bfloat16), jnp.zeros(shape, jnp.bfloat16)
 
     received = jnp.zeros((length, model), jnp.bfloat16)
@@ -374,12 +373,20 @@
         arrived = lax.all_to_all(
             forward_outgoing, EXPERT, split_axis=0, concat_axis=0, tiled=True
         ).reshape(owners, local, capacity, model)
-        tick_up, tick_down = (early_w, early_down) if tick == 0 else (up_w, down_w)
-        before = jnp.einsum("secd,edf->secf", arrived, tick_up, preferred_element_type=jnp.float32)
+        if tick == 0:
+            early_w, arrived = lax.optimization_barrier((early_w, arrived))
+            early_down = lax.ppermute(early_w, SECTION, [(1, 0)])
+            up_w, down_w = early_w, early_down
+        elif tick == 1:
+            late_w, arrived = lax.optimization_barrier((late_w, arrived))
+            late_down = lax.ppermute(late_w, SECTION, [(0, 1)])
+            up_w = jnp.where(first, early_w, late_w)
+            down_w = jnp.where(first, early_down, late_down)
+        before = jnp.einsum("secd,edf->secf", arrived, up_w, preferred_element_type=jnp.float32)
         activated, slope = gelu_both(before)
         activated, slope = lax.optimization_barrier((activated, slope))
         after = jnp.einsum(
-            "secf,edf->secd", activated, tick_down, preferred_element_type=jnp.float32
+            "secf,edf->secd", activated, down_w, preferred_element_type=jnp.float32
         ).astype(jnp.bfloat16)
         returned = lax.all_to_all(
             after.reshape(owners, local * capacity, model),
@@ -445,15 +452,16 @@
             "secd,edf->secf", arrived_grad, down_w, preferred_element_type=jnp.float32
         )
         before_grad = (activation_grad * kept.slope.astype(jnp.float32)).astype(jnp.bfloat16)
+        if tick == batches:
+            early_sum, arrived_grad = lax.optimization_barrier((early_sum, arrived_grad))
+            early_share = scatter(early_sum)
         expert_steps.append(ExpertStep(kept.arrived, kept.activated, arrived_grad, before_grad))
         if tick == batches:
             expert_sums = lax.cond(first, later_sums, empty_sums, *expert_steps[1:])
             kept_sums, before_grad = lax.optimization_barrier((expert_sums, before_grad))
             up_sum, down_sum = kept_sums
             swapped = lax.ppermute(down_sum, SECTION, [(0, 1)])
-            late_share = lax.psum_scatter(
-                jnp.where(first, up_sum, swapped), DP, scatter_dimension=1, tiled=True
-            )
+            late_sum = jnp.where(first, up_sum, swapped)
         input_rows_grad = jnp.einsum(
             "secf,edf->secd", before_grad, up_w, preferred_element_type=jnp.float32
         ).astype(jnp.bfloat16)
@@ -487,6 +495,11 @@
             kept.projected, mixed_grad, relative, kept.segment
         )
         projected_grad = jnp.concatenate(projected_grad, 1)
+        if tick == batches:
+            early_share, late_sum, projected_grad = lax.optimization_barrier(
+                (early_share, late_sum, projected_grad)
+            )
+            late_share = scatter(late_sum)
         normed_grad = jnp.einsum(
             "le,ce->lc", projected_grad, qkv_w, preferred_element_type=jnp.float32
         )
@@ -509,35 +522,17 @@
         if tick < batches:
             arriving = from_behind(results[-1], SECTION, -1)
         if tick == batches - 1:
-            up_sum, down_sum = lax.cond(first, empty_sums, later_sums, *expert_steps)
-            swapped = lax.ppermute(up_sum, SECTION, [(1, 0)])
-            early_share = lax.psum_scatter(
-                jnp.where(first, swapped, down_sum), DP, scatter_dimension=1, tiled=True
-            )
+            early_sums = lax.cond(first, empty_sums, later_sums, *expert_steps)
+            early_sums, arriving = lax.optimization_barrier((early_sums, arriving))
+            up_sum, down_sum = early_sums
+            swapped = lax.ppermute(down_sum, SECTION, [(1, 0)])
+            early_sum = jnp.where(first, swapped, up_sum)
     blocks = [jnp.where(first, results[index + 1], produced[index + 1]) for index in range(batches)]
     ends_out = jnp.concatenate(blocks, 0)[None]
     parts = merged(steps)
     score_pairs = [part.score_grad for part in parts]
     offsets = offset_sums(score_pairs[0], score_pairs[1])
     table_sum = jnp.dot(bucket_hot, offsets.T, precision=highest)
-    projection_sum = jnp.concatenate(
-        [
-            product([part.normed for part in parts], [part.projected_grad for part in parts]),
-            product([part.mixed for part in parts], [part.branch_grad for part in parts]),
-        ],
-        1,
-    ).reshape(layers, owners, piece, 4 * model)
-    quarters = lax.all_to_all(projection_sum, EXPERT, split_axis=1, concat_axis=1, tiled=True)
-    quarter = quarters.astype(jnp.float32).sum(1).astype(jnp.bfloat16)
-    share = lax.psum_scatter(
-        quarter.reshape(layers * piece, 4 * model), DP, scatter_dimension=0, tiled=True
-    )
-    shares = spread(share).reshape(owners * piece, 4 * model).astype(jnp.float32)
-    exchanged = lax.ppermute(
-        jnp.where(first, early_share, late_share), SECTION, [(0, 1), (1, 0)]
-    )
-    up_share = jnp.where(first, late_share, exchanged).reshape(experts_up.shape)
-    down_share = jnp.where(first, exchanged, early_share).reshape(local, -1, up_w.shape[2])
     small_sum = jnp.concatenate(
         [
             sum(part.gain_one for part in parts).reshape(layers, -1),
@@ -547,9 +542,32 @@
         ],
         1,
     ).astype(jnp.bfloat16)
-    small_share = lax.dynamic_index_in_dim(
-        lax.psum(small_sum, (DP, EXPERT)), lax.axis_index(DP), 0, keepdims=False
-    ).astype(jnp.float32)
+    extra = 8 - piece % 8
+    lines = jnp.pad(small_sum, ((0, 0), (0, extra * 4 * model - small_sum.shape[1])))
+    lines = jnp.broadcast_to(
+        lines.reshape(layers, 1, extra, 4 * model), (layers, owners, extra, 4 * model)
+    )
+    projection_sum = jnp.concatenate(
+        [
+            product([part.normed for part in parts], [part.projected_grad for part in parts]),
+            product([part.mixed for part in parts], [part.branch_grad for part in parts]),
+        ],
+        1,
+    ).reshape(layers, owners, piece, 4 * model)
+    projection_sum = jnp.concatenate([projection_sum, lines], 2)
+    quarters = lax.all_to_all(projection_sum, EXPERT, split_axis=1, concat_axis=1, tiled=True)
+    quarter = quarters.astype(jnp.float32).sum(1).astype(jnp.bfloat16)
+    late_share, quarter = lax.optimization_barrier((late_share, quarter))
+    share = lax.psum_scatter(
+        quarter.reshape(layers * (piece + extra), 4 * model), DP, scatter_dimension=0, tiled=True
+    )
+    shares = spread(share[:piece]).reshape(owners * piece, 4 * model).astype(jnp.float32)
+    small_share = share[piece:].reshape(-1).astype(jnp.float32)
+    exchanged = lax.ppermute(
+        jnp.where(first, early_share, late_share), SECTION, [(0, 1), (1, 0)]
+    )
+    up_share = jnp.where(first, late_share, early_share).reshape(experts_up.shape)
+    down_share = exchanged.reshape(local, -1, own_up.shape[2])
     return (
         ends_out,
         shares[None, :, :model],
@@ -559,7 +577,7 @@
         small_share[None, :rows],
         small_share[None, rows : 2 * rows],
         small_share[2 * rows : (2 + kinds) * rows].reshape(1, rows, kinds),
-        small_share[(2 + kinds) * rows :].reshape(1, -1, bias_table.shape[2]),
+        small_share[(2 + kinds) * rows : small_sum.shape[1]].reshape(1, -1, bias_table.shape[2]),
         up_share.astype(jnp.float32),
         jnp.swapaxes(down_share.astype(jnp.float32), 1, 2)[None],
     )

time: 920 us -> 771 us (0.84)
  local copies, waits for them, and re-layouts: 183 us -> 70.3 us
  waiting for transfers between devices: 243 us -> 199 us
  matrix products: 160 us -> 173 us
    unnamed x211 -> x269, local copies, waits for them, and re-layouts: 126 us -> 27.2 us
    all_to_all x0 -> x2, blocking collectives: none -> 80.1 us  [the longest x1 66.1 us: shards(): lax.all_to_all(projection_sum, EXPERT, split_axis=1, concat_axis=1, tiled...]
    psum x1 -> x0, blocking collectives: 76.2 us -> none  [shards(): lax.psum(small_sum, (DP, EXPERT))]
    all_gather x1, waiting for transfers between devices: 65.7 us -> 0.01 us  [shards(): lax.all_gather(jnp.where(first, own_up, swapped), DP, axis=1, tiled=True)]
    all_to_all x2, waiting for transfers between devices: 0.01 us -> 40.6 us  [spread(): lax.all_to_all(jnp.broadcast_to(block[None], (owners, *block.shape)), EXP...]
    all_gather x1, waiting for transfers between devices: 63.4 us -> 26.2 us  [shards(): lax.all_gather(jnp.where(first, swapped, own_up), DP, axis=1, tiled=True)]
    ppermute x3, waiting for transfers between devices: 2.61 us -> 35.6 us  [the longest x1 32.9 us: shards(): swapped = lax.ppermute(down_sum, SECTION, [(1, 0)])]
    reduce_scatter x1 -> x3, waiting for transfers between devices: 0.02 us -> 29.5 us  [the longest x1 23.9 us: shards(): lax.psum_scatter(quarter.reshape(layers * (piece + extra), 4 * model), DP...]
  transfers between devices with their start and end apart: 30 -> 28, of which waited for: 18 -> 18; matrix products, arithmetic and copies ran while one was open for 27% -> 27% of each run, Pallas kernels for 3% -> 5%
where the time goes in v2:
time: 771 us; the launch traced here: 759 us
  waiting for transfers between devices  199 us (26%)
  matrix products  173 us (22%)
  blocking collectives  106 us (14%)
  starting transfers between devices  72 us (9%)
  local copies, waits for them, and re-layouts  70.3 us (9%)
  Pallas kernels  65.1 us (8%)
  other arithmetic  56.8 us (7%)
  between operations  16.5 us (2%)
    all_to_all x1, blocking collectives, shards(): lax.all_to_all(projection_sum, EXPERT, split_axis=1, concat_axis=1, tiled...  66.1 us
    all_to_all x2, waiting for transfers between devices, spread(): lax.all_to_all(jnp.broadcast_to(block[None], (owners, *block.shape)), EXP...  40.6 us
    ppermute x1, waiting for transfers between devices, shards(): swapped = lax.ppermute(down_sum, SECTION, [(1, 0)])  32.9 us
    dot_general x8, matrix products, product(): lax.dot_general(left, right, (((0,), (0,)), ((), ())), preferred_element_...  32.3 us
    all_gather x1, waiting for transfers between devices, shards(): lax.all_gather(lax.dynamic_slice_in_dim(projections, mine * piece, piece,...  31.1 us
    pallas_call x3, Pallas kernels, attend_back(): pl.pallas_call(functools.partial(backward_body, model // heads), grid=(gr...  27.9 us
    unnamed x269, local copies, waits for them, and re-layouts  27.2 us
    all_gather x1, waiting for transfers between devices, shards(): lax.all_gather(jnp.where(first, swapped, own_up), DP, axis=1, tiled=True)  26.2 us
  transfers between devices with their start and end apart: 28, of which 18 were waited for; matrix products, arithmetic and copies ran while one was open for 27% of the time, Pallas kernels for 5%

profile of v2, /device:TPU:0, one launch (start us, length us, event | category | flops | bytes accessed | tf_op | source)
XLA Modules:
  0.0 759.4 jit_solution(15818624234505849628)
XLA Ops:
  12.2 31.1 %all-gather.10.cloned.1.call-done = bf16[192,3072]{1,0:T(8,128)(2,1)} async-done(((bf16[48,3072]{1,0:T(8,128)(2,1)}), bf16[192,3072]{1,0:T(8,128)(2,1)}) %all-gather.10.cloned.1.call-update) | async-done | bytes 1179664 | tf_op jit(solution)/shard_map/all_gather | solution.py:251
  49.1 5.2 all-to-all-start
  54.9 13.4 %all-gather.1 = bf16[4,1,1248]{2,1,0:T(2,128)(2,1)S(1)} all-gather(bf16[1,1,1248]{2,1,0:T(2,128)(2,1)S(1)} %bitcast.535), channel_id=1, replica_groups=mesh['section'=2,'dp'=4,'expert'=4] {'dp'}, dimensions={0}, use_global_device_ids=true | all-gather | bytes 12480 | tf_op jit(solution)/shard_map/all_gather | solution.py:264
  69.9 7.0 spread_offsets.1.bias
  77.2 29.7 %all-to-all-done = bf16[4,4,48,3072]{3,2,1,0:T(8,128)(2,1)} async-done(((bf16[4,4,48,3072]{3,2,1,0:T(8,128)(2,1)}), bf16[4,4,48,3072]{3,2,1,0:T(8,128)(2,1)}, u32[]{:S(2)}, u32[]{:S(2)}) %all-to-all-start) | async-done | bytes 4718624 | tf_op jit(solution)/shard_map/all_to_all | solution.py:256
  113.8 7.0 attend.3
  123.7 13.9 %all_to_all.75 = bf16[4,128,768]{2,1,0:T(8,128)(2,1)} all-to-all(bf16[4,128,768]{2,1,0:T(8,128)(2,1)S(1)} %bitcast.506), channel_id=1, replica_groups=mesh['section'=2,'dp'=4,'expert'=4] {'expert'}, dimensions={0} | all-to-all | bytes 1572864 | tf_op jit(solution)/shard_map/all_to_all | solution.py:373
  139.0 8.3 %fusion.25 = (bf16[4,1,128,3072]{2,3,0,1:T(8,128)(2,1)}, bf16[4,1,128,3072]{2,3,0,1:T(8,128)(2,1)S(1)}) fusion(bf16[4,1,128,768]{3,2,0,1:T(8,128)(2,1)} %bitcast.496, bf16[1,768,3072]{2,1,0:T(8,128)(2,1)} %all-gather.6.cloned.1.call-done), kind=kOutput, calls=%fused_computation.35 | convolution fusion | flops 2433220608 | bytes 11796480 | tf_op jit(solution)/shard_map/secd,edf->secf/dot_general | solution.py:385
  148.9 6.2 fusion.140
  155.1 4.2 all-to-all-start.2
  161.2 9.3 %all-to-all-done.2 = bf16[4,128,768]{1,2,0:T(8,128)(2,1)} async-done(((bf16[4,128,768]{1,2,0:T(8,128)(2,1)}), bf16[4,128,768]{1,2,0:T(8,128)(2,1)}, u32[]{:S(2)}, u32[]{:S(2)}) %all-to-all-start.2) | async-done | bytes 786464 | tf_op jit(solution)/shard_map/all_to_all | solution.py:391
  175.5 4.1 collective-permute-start.2
  184.9 7.0 attend.4
  199.4 4.2 all-to-all-start.3
  203.6 26.2 %all-gather.8.cloned.1.call-done = bf16[1,768,3072]{2,1,0:T(8,128)(2,1)} async-done(((bf16[1,192,3072]{2,1,0:T(8,128)(2,1)}), bf16[1,768,3072]{2,1,0:T(8,128)(2,1)}) %all-gather.8.cloned.1.call-update) | async-done | bytes 4718608 | tf_op jit(solution)/shard_map/all_gather | solution.py:276
  229.8 4.0 collective-permute-start.3
  237.6 4.2 all-to-all-start.4
  244.6 8.0 %fusion.30 = (bf16[4,1,128,3072]{2,3,0,1:T(8,128)(2,1)}, bf16[4,1,128,3072]{2,3,0,1:T(8,128)(2,1)S(1)}) fusion(bf16[4,1,128,768]{2,3,0,1:T(8,128)(2,1)} %bitcast.63, bf16[1,768,3072]{2,1,0:T(8,128)(2,1)S(1)} %broadcast_select_fusion.3), kind=kOutput, calls=%fused_computation.40 | convolution fusion | flops 2433220608 | bytes 11796480 | tf_op jit(solution)/shard_map/secd,edf->secf/dot_general | solution.py:385
  252.7 4.0 broadcast_select_fusion.2
  262.3 4.2 all-to-all-start.6
  266.5 6.0 fusion.19
  274.1 5.8 fusion.135
  280.0 4.6 all-to-all-start.5
  295.4 4.0 multiply_reduce_fusion
  305.4 4.4 broadcast_select_fusion.6
  309.8 7.0 attend.5
  318.3 9.3 %attend_back.3 = (bf16[256,768]{1,0:T(8,128)(2,1)S(1)}, bf16[256,768]{1,0:T(8,128)(2,1)S(1)}, bf16[256,768]{1,0:T(8,128)(2,1)S(1)}, bf16[12,256,256]{2,1,0:T(8,128)(2,1)S(1)}) custom-call(s32[256,1]{1,0:T(8,128)S(1)} %copy.102.column, s32[1,256]{1,0:T(1,128)S(1)} %bitcast.464, bf16[256,2304]{1,0:T(8,128)(2,1)S(1)} %copy-done.2, ...), custom_call_target="tpu_custom_call" | custom-call | tf_op jit(solution)/shard_map/attend_back/pallas_call | solution.py:179
  334.0 4.4 all-to-all-start.8
  342.1 5.0 fusion.155
  350.2 8.3 %fusion.35 = (bf16[4,1,128,3072]{2,3,0,1:T(8,128)(2,1)}, bf16[4,1,128,3072]{2,3,0,1:T(8,128)(2,1)S(1)}) fusion(bf16[4,128,768]{2,1,0:T(8,128)(2,1)} %all-to-all-done.8, bf16[1,768,3072]{2,1,0:T(8,128)(2,1)} %copy-done.43), kind=kOutput, calls=%fused_computation.45 | convolution fusion | flops 2433220608 | bytes 11796480 | tf_op jit(solution)/shard_map/secd,edf->secf/dot_general | solution.py:385
  360.3 5.9 fusion.115
  366.1 4.2 all-to-all-start.10
  375.5 5.8 all-to-all-done.10
  388.3 12.9 %all_to_all.76 = bf16[4,128,768]{2,1,0:T(8,128)(2,1)S(1)} all-to-all(bf16[4,128,768]{2,1,0:T(8,128)(2,1)S(1)} %bitcast.516), channel_id=1, replica_groups=mesh['section'=2,'dp'=4,'expert'=4] {'expert'}, dimensions={0} | all-to-all | bytes 1572864 | tf_op jit(solution)/shard_map/all_to_all | solution.py:448
  401.2 6.0 fusion.36
  412.4 4.6 all-to-all-start.9
  417.2 8.3 %all-to-all-done.9 = bf16[4,128,768]{1,2,0:T(8,128)(2,1)} async-done(((bf16[4,128,768]{1,2,0:T(8,128)(2,1)}), bf16[4,128,768]{1,2,0:T(8,128)(2,1)}, u32[]{:S(2)}, u32[]{:S(2)}) %all-to-all-start.9) | async-done | bytes 786464 | tf_op jit(solution)/shard_map/all_to_all | solution.py:468
  435.8 9.3 %attend_back.4 = (bf16[256,768]{1,0:T(8,128)(2,1)S(1)}, bf16[256,768]{1,0:T(8,128)(2,1)S(1)}, bf16[256,768]{1,0:T(8,128)(2,1)S(1)}, bf16[12,256,256]{2,1,0:T(8,128)(2,1)S(1)}) custom-call(s32[256,1]{1,0:T(8,128)S(1)} %copy.119.column, s32[1,256]{1,0:T(1,128)S(1)} %bitcast.467, bf16[256,2304]{1,0:T(8,128)(2,1)S(1)} %copy-done.6, ...), custom_call_target="tpu_custom_call" | custom-call | tf_op jit(solution)/shard_map/attend_back/pallas_call | solution.py:179
  454.2 5.5 conditional.2
  464.6 4.2 all-to-all-start.11
  469.0 32.9 %collective-permute-done.7 = bf16[1,768,3072]{2,1,0:T(8,128)(2,1)} collective-permute-done((bf16[1,768,3072]{2,1,0:T(8,128)(2,1)}, bf16[1,768,3072]{2,1,0:T(8,128)(2,1)}, u32[]{:S(2)}, u32[]{:S(2)}) %collective-permute-start.7) | collective-permute-done | bytes 4718624 | tf_op jit(solution)/shard_map/ppermute | solution.py:528
  502.0 5.0 broadcast_select_fusion.1
  507.0 6.1 fusion.20
  514.9 24.8 %conditional.3 = (bf16[1,768,3072]{2,1,0:T(8,128)(2,1)}, bf16[1,768,3072]{2,1,0:T(8,128)(2,1)}) conditional(s32[]{:T(128)} %convert_element_type.395, () %tuple.44, (bf16[4,1,128,768]{3,2,0,1:T(8,128)(2,1)}, bf16[4,1,128,3072]{2,3,0,1:T(8,128)(2,1)S(1)}, bf16[4,1,128,768]{2,3,0,1:T(8,128)(2,1)}, bf16[4,1,128,3072]{2,3,0,1:T(8,128)(2,1)S(1)}, ...), branch_computations={%region_25.26_spmd, %region_26.27_spmd} | conditional | flops 9673113600 | bytes 81788976 | solution.py:460
  514.9 3.9 fusion.14
  518.8 5.5 fusion.10
  524.4 4.7 copy.129
  529.0 5.0 fusion.302
  534.1 5.7 fusion.11
  543.3 6.8 fusion.125
  550.1 4.2 all-to-all-start.12
  556.7 5.6 all-to-all-done.12
  571.6 9.3 %attend_back.5 = (bf16[256,768]{1,0:T(8,128)(2,1)S(1)}, bf16[256,768]{1,0:T(8,128)(2,1)S(1)}, bf16[256,768]{1,0:T(8,128)(2,1)S(1)}, bf16[12,256,256]{2,1,0:T(8,128)(2,1)S(1)}) custom-call(s32[256,1]{1,0:T(8,128)S(1)} %copy.102.column, s32[1,256]{1,0:T(1,128)S(1)} %bitcast.465, bf16[256,2304]{1,0:T(8,128)(2,1)S(1)} %copy-done.3, ...), custom_call_target="tpu_custom_call" | custom-call | tf_op jit(solution)/shard_map/attend_back/pallas_call | solution.py:179
  583.1 4.9 broadcast_select_fusion
  588.1 5.6 reduce-scatter.4.cloned.1.call-done
  594.5 5.8 fusion.201
  603.2 9.2 %offset_sums.1 = f32[12,1,512]{2,1,0:T(1,128)} custom-call(bf16[12,256,256]{2,1,0:T(8,128)(2,1)} %copy-done.11, bf16[12,256,256]{2,1,0:T(8,128)(2,1)} %broadcast_select_fusion.5.two), custom_call_target="tpu_custom_call" | custom-call | tf_op jit(solution)/shard_map/offset_sums/pallas_call | solution.py:205
  615.8 4.7 fusion.154
  620.9 4.3 add_convert_fusion.1
  626.7 66.1 %all_to_all.77 = bf16[4,4,56,3072]{3,2,0,1:T(8,128)(2,1)} all-to-all(bf16[4,4,56,3072]{3,2,0,1:T(8,128)(2,1)S(1)} %pad_maximum_fusion), channel_id=1, replica_groups=mesh['section'=2,'dp'=4,'expert'=4] {'expert'}, dimensions={1} | all-to-all | bytes 11010048 | tf_op jit(solution)/shard_map/all_to_all | solution.py:558
  692.8 5.2 reduce_sum.317
  705.7 23.9 %reduce-scatter.8.cloned.1.call-done = bf16[56,3072]{1,0:T(8,128)(2,1)} async-done(((bf16[224,3072]{1,0:T(8,128)(2,1)}), bf16[56,3072]{1,0:T(8,128)(2,1)}) %reduce-scatter.8.cloned.1.call-update) | async-done | bytes 344080 | tf_op jit(solution)/shard_map/reduce_scatter | solution.py:561
  731.7 3.6 all-to-all-start.14
  739.4 10.9 %all-to-all-done.14 = bf16[4,48,3072]{2,1,0:T(8,128)(2,1)S(1)} async-done(((bf16[4,48,3072]{2,1,0:T(8,128)(2,1)}), bf16[4,48,3072]{2,1,0:T(8,128)(2,1)S(1)}, u32[]{:S(2)}, u32[]{:S(2)}) %all-to-all-start.14) | async-done | bytes 1179680 | tf_op jit(solution)/shard_map/all_to_all | solution.py:256
  (450 shorter events, 182.7 us)
Async XLA Ops:
  7.2 36.2 %all-gather.10.cloned.1.call-start = ((), (), s32[]{:S(2)}) async-start(), calls=%async_computation.23 | async-start | bytes 1474560 | tf_op jit(solution)/shard_map/all_gather | solution.py:251
  9.0 128.7 %all-gather.6.cloned.1.call-start = ((), (), s32[]{:S(2)}) async-start(), calls=%async_computation.18 | async-start | bytes 5898240 | tf_op jit(solution)/shard_map/all_gather | solution.py:275
  9.0 3.2 collective-permute-start
  49.1 19.4 %copy-start.113 = (s32[512]{0:T(512)S(1)}, s32[512]{0:T(512)}, u32[]{:S(2)}) copy-start(s32[512]{0:T(512)} %param.32) | copy-start | bytes 6148
  49.1 19.8 %slice-start.6 = ((s32[511]{0:T(512)}), s32[256]{0:T(256)S(1)}, s32[]{:S(2)}) async-start(s32[511]{0:T(512)} %param.33), calls=%async_computation.30 | async-start | bytes 2048 | tf_op jit(solution)/shard_map/slice | solution.py:288
  49.1 57.8 %all-to-all-start = ((bf16[4,4,48,3072]{3,2,1,0:T(8,128)(2,1)}), bf16[4,4,48,3072]{3,2,1,0:T(8,128)(2,1)}, u32[]{:S(2)}, u32[]{:S(2)}) async-start(bf16[4,4,48,3072]{3,2,1,0:T(8,128)(2,1)} %broadcast_in_dim.63), calls=%async_computation | async-start | bytes 9437184 | tf_op jit(solution)/shard_map/all_to_all | solution.py:256
  54.3 22.6 %copy-start.29 = (bf16[1,512,768]{2,1,0:T(8,128)(2,1)S(1)}, bf16[1,512,768]{2,1,0:T(8,128)(2,1)}, u32[]{:S(2)}) copy-start(bf16[1,512,768]{2,1,0:T(8,128)(2,1)} %param.19) | copy-start | bytes 2359300
  54.3 22.8 %copy-start.110 = (s32[1,512]{1,0:T(1,128)S(1)}, s32[1,512]{1,0:T(1,128)}, u32[]{:S(2)}) copy-start(s32[1,512]{1,0:T(1,128)} %param.31) | copy-start | bytes 6148
  54.3 22.8 %copy-start.111 = (s32[1,512]{1,0:T(1,128)S(1)}, s32[1,512]{1,0:T(1,128)}, u32[]{:S(2)}) copy-start(s32[1,512]{1,0:T(1,128)} %param.30) | copy-start | bytes 6148
  54.3 175.5 %all-gather.8.cloned.1.call-start = ((), (), s32[]{:S(2)}) async-start(), calls=%async_computation.19 | async-start | bytes 5898240 | tf_op jit(solution)/shard_map/all_gather | solution.py:276
  77.2 32.6 %copy-start.96 = (f32[256]{0:T(256)}, f32[256]{0:T(256)S(1)}, u32[]{:S(2)}) copy-start(f32[256]{0:T(256)S(1)} %add_rsqrt_fusion.3) | copy-start | bytes 3076
  109.8 11.0 %copy-start.22 = (bf16[4,4,48,3072]{3,2,0,1:T(8,128)(2,1)}, bf16[4,4,48,3072]{3,2,0,1:T(8,128)(2,1)S(1)}, u32[]{:S(2)}) copy-start(bf16[4,4,48,3072]{3,2,0,1:T(8,128)(2,1)S(1)} %copy.97) | copy-start | bytes 14155780
  137.7 10.1 %collective-permute-start.1 = (bf16[1,768,3072]{2,1,0:T(8,128)(2,1)}, bf16[1,768,3072]{2,1,0:T(8,128)(2,1)}, u32[]{:S(2)}, u32[]{:S(2)}) collective-permute-start(bf16[1,768,3072]{2,1,0:T(8,128)(2,1)} %all-gather.6.cloned.1.call-done), channel_id=1, source_target_pairs={{16,0},{17,1},{18,2},{19,3},{20,4},{21,5},{22,6},{23,7},{24,8},{25... | collective-permute-start | bytes 14155784 | tf_op jit(solution)/shard_map/ppermute | solution.py:378
  155.1 15.4 %all-to-all-start.2 = ((bf16[4,128,768]{1,2,0:T(8,128)(2,1)}), bf16[4,128,768]{1,2,0:T(8,128)(2,1)}, u32[]{:S(2)}, u32[]{:S(2)}) async-start(bf16[4,128,768]{1,2,0:T(8,128)(2,1)} %fusion.140), calls=%async_computation.2 | async-start | bytes 1572864 | tf_op jit(solution)/shard_map/all_to_all | solution.py:391
  159.8 19.8 %copy-start.34 = (bf16[768,4]{1,0:T(8,128)(2,1)}, bf16[768,4]{1,0:T(8,128)(2,1)S(1)}, u32[]{:S(2)}) copy-start(bf16[768,4]{1,0:T(8,128)(2,1)S(1)} %reshape.500) | copy-start | bytes 18436
  161.1 268.3 %copy-start.80 = (f32[256]{0:T(256)}, f32[256]{0:T(256)S(1)}, u32[]{:S(2)}) copy-start(f32[256]{0:T(256)S(1)} %get-tuple-element.280) | copy-start | bytes 3076
  161.2 268.2 %copy-start.90 = (f32[256]{0:T(256)}, f32[256]{0:T(256)S(1)}, u32[]{:S(2)}) copy-start(f32[256]{0:T(256)S(1)} %fusion.252) | copy-start | bytes 3076
  175.5 4.8 collective-permute-start.2
  181.6 188.8 %copy-start.75 = (f32[256]{0:T(256)}, f32[256]{0:T(256)S(1)}, u32[]{:S(2)}) copy-start(f32[256]{0:T(256)S(1)} %fusion.278) | copy-start | bytes 3076
  199.4 30.4 %all-to-all-start.3 = ((bf16[4,128,768]{1,2,0:T(8,128)(2,1)}), bf16[4,128,768]{1,2,0:T(8,128)(2,1)}, u32[]{:S(2)}, u32[]{:S(2)}) async-start(bf16[4,128,768]{1,2,0:T(8,128)(2,1)} %copy.103), calls=%async_computation.3 | async-start | bytes 1572864 | tf_op jit(solution)/shard_map/all_to_all | solution.py:373
  229.8 22.8 %collective-permute-start.3 = (bf16[1,768,3072]{2,1,0:T(8,128)(2,1)}, bf16[1,768,3072]{2,1,0:T(8,128)(2,1)}, u32[]{:S(2)}, u32[]{:S(2)}) collective-permute-start(bf16[1,768,3072]{2,1,0:T(8,128)(2,1)} %all-gather.8.cloned.1.call-done), channel_id=1, source_target_pairs={{0,16},{1,17},{2,18},{3,19},{4,20},{5,21},{6,22},{7,23},{8,24},{9,... | collective-permute-start | bytes 14155784 | tf_op jit(solution)/shard_map/ppermute | solution.py:382
  233.9 195.6 %copy-start.100 = (s32[256]{0:T(256)}, s32[256]{0:T(256)S(1)}, u32[]{:S(2)}) copy-start(s32[256]{0:T(256)S(1)} %get-tuple-element.274) | copy-start | bytes 3076
  233.9 320.5 %copy-start.70 = (s32[256]{0:T(256)}, s32[256]{0:T(256)S(1)}, u32[]{:S(2)}) copy-start(s32[256]{0:T(256)S(1)} %get-tuple-element.275) | copy-start | bytes 3076
  237.6 24.7 %all-to-all-start.4 = ((bf16[4,128,768]{2,1,0:T(8,128)(2,1)}), bf16[4,128,768]{2,1,0:T(8,128)(2,1)}, u32[]{:S(2)}, u32[]{:S(2)}) async-start(bf16[4,128,768]{2,1,0:T(8,128)(2,1)} %bitcast.512), calls=%async_computation.4 | async-start | bytes 1572864 | tf_op jit(solution)/shard_map/all_to_all | solution.py:448
  262.3 17.7 %all-to-all-start.6 = ((bf16[4,128,768]{1,2,0:T(8,128)(2,1)}), bf16[4,128,768]{1,2,0:T(8,128)(2,1)}, u32[]{:S(2)}, u32[]{:S(2)}) async-start(bf16[4,128,768]{1,2,0:T(8,128)(2,1)} %fusion.120), calls=%async_computation.6 | async-start | bytes 1572864 | tf_op jit(solution)/shard_map/all_to_all | solution.py:391
  280.0 13.2 %all-to-all-start.5 = ((bf16[4,128,768]{1,2,0:T(8,128)(2,1)}), bf16[4,128,768]{1,2,0:T(8,128)(2,1)}, u32[]{:S(2)}, u32[]{:S(2)}) async-start(bf16[4,128,768]{1,2,0:T(8,128)(2,1)} %fusion.135), calls=%async_computation.5 | async-start | bytes 1572864 | tf_op jit(solution)/shard_map/all_to_all | solution.py:468
  289.4 15.7 %copy-start.84 = (f32[256]{0:T(256)}, f32[256]{0:T(256)S(1)}, u32[]{:S(2)}) copy-start(f32[256]{0:T(256)S(1)} %get-tuple-element.288) | copy-start | bytes 3076
  289.4 15.7 %copy-start.86 = (f32[256]{0:T(256)}, f32[256]{0:T(256)S(1)}, u32[]{:S(2)}) copy-start(f32[256]{0:T(256)S(1)} %mul.594) | copy-start | bytes 3076
  299.4 3.0 collective-permute-start.5
  302.4 14.4 %slice-start = ((s8[4718592]{0:T(1024)(128)(4,1)}), s8[4194304]{0:T(1024)(128)(4,1)S(1)}, s32[]{:S(2)}) async-start(s8[4718592]{0:T(1024)(128)(4,1)} %bitcast.484), calls=%async_computation.24 | async-start | bytes 8388608
  305.2 11.6 %copy-start.45 = (bf16[256,768]{1,0:T(8,128)(2,1)}, bf16[256,768]{1,0:T(8,128)(2,1)S(1)}, u32[]{:S(2)}) copy-start(bf16[256,768]{1,0:T(8,128)(2,1)S(1)} %get-tuple-element.231) | copy-start | bytes 1179652
  305.2 12.3 %copy-start.25 = (f32[256,768]{1,0:T(8,128)}, f32[256,768]{1,0:T(8,128)S(1)}, u32[]{:S(2)}) copy-start(f32[256,768]{1,0:T(8,128)S(1)} %get-tuple-element.259) | copy-start | bytes 2359300
  305.4 11.5 %slice-start.1 = ((s8[4718592]{0:T(1024)(128)(4,1)}), s8[524288]{0:T(1024)(128)(4,1)S(1)}, s32[]{:S(2)}) async-start(s8[4718592]{0:T(1024)(128)(4,1)} %bitcast.484), calls=%async_computation.25 | async-start | bytes 1048576
  317.4 13.6 %copy-start.60 = (f32[256,768]{1,0:T(8,128)}, f32[256,768]{1,0:T(8,128)S(1)}, u32[]{:S(2)}) copy-start(f32[256,768]{1,0:T(8,128)S(1)} %get-tuple-element.292) | copy-start | bytes 2359300
  318.3 12.8 %copy-start.36 = (f32[256,768]{1,0:T(8,128)S(1)}, f32[256,768]{1,0:T(8,128)}, u32[]{:S(2)}) copy-start(f32[256,768]{1,0:T(8,128)} %copy-done.35) | copy-start | bytes 2359300
  334.0 16.2 %all-to-all-start.8 = ((bf16[4,128,768]{2,1,0:T(8,128)(2,1)}), bf16[4,128,768]{2,1,0:T(8,128)(2,1)}, u32[]{:S(2)}, u32[]{:S(2)}) async-start(bf16[4,128,768]{2,1,0:T(8,128)(2,1)} %bitcast.503), calls=%async_computation.8 | async-start | bytes 1572864 | tf_op jit(solution)/shard_map/all_to_all | solution.py:373
  366.1 15.2 %all-to-all-start.10 = ((bf16[4,128,768]{1,2,0:T(8,128)(2,1)}), bf16[4,128,768]{1,2,0:T(8,128)(2,1)}, u32[]{:S(2)}, u32[]{:S(2)}) async-start(bf16[4,128,768]{1,2,0:T(8,128)(2,1)} %fusion.115), calls=%async_computation.10 | async-start | bytes 1572864 | tf_op jit(solution)/shard_map/all_to_all | solution.py:391
  372.8 10.8 %collective-permute-start.4 = (bf16[256,768]{1,0:T(8,128)(2,1)}, bf16[256,768]{1,0:T(8,128)(2,1)}, u32[]{:S(2)}, u32[]{:S(2)}) collective-permute-start(bf16[256,768]{1,0:T(8,128)(2,1)} %fusion.160), channel_id=1, source_target_pairs={{16,0},{17,1},{18,2},{19,3},{20,4},{21,5},{22,6},{23,7},{24,8},{25... | collective-permute-start | bytes 1179656 | tf_op jit(solution)/shard_map/ppermute | solution.py:55
  375.4 54.0 %copy-start.82 = (f32[256]{0:T(256)}, f32[256]{0:T(256)S(1)}, u32[]{:S(2)}) copy-start(f32[256]{0:T(256)S(1)} %get-tuple-element.296) | copy-start | bytes 3076
  375.5 54.0 %copy-start.94 = (f32[256]{0:T(256)}, f32[256]{0:T(256)S(1)}, u32[]{:S(2)}) copy-start(f32[256]{0:T(256)S(1)} %fusion.256) | copy-start | bytes 3076
  375.5 25.7 %copy-start.92 = (f32[256]{0:T(256)}, f32[256]{0:T(256)S(1)}, u32[]{:S(2)}) copy-start(f32[256]{0:T(256)S(1)} %select_reduce_fusion) | copy-start | bytes 3076
  383.7 17.5 %copy-start.122 = (bf16[4,1,128,3072]{2,3,0,1:T(8,128)(2,1)S(1)}, bf16[4,1,128,3072]{2,3,0,1:T(8,128)(2,1)}, u32[]{:S(2)}) copy-start(bf16[4,1,128,3072]{2,3,0,1:T(8,128)(2,1)} %get-tuple-element.114) | copy-start | bytes 9437188
  383.7 17.5 %copy-start.123 = (bf16[4,1,128,3072]{2,3,0,1:T(8,128)(2,1)S(1)}, bf16[4,1,128,3072]{2,3,0,1:T(8,128)(2,1)}, u32[]{:S(2)}) copy-start(bf16[4,1,128,3072]{2,3,0,1:T(8,128)(2,1)} %get-tuple-element.115) | copy-start | bytes 9437188
  386.5 43.0 %copy-start.102 = (f32[256]{0:T(256)}, f32[256]{0:T(256)S(1)}, u32[]{:S(2)}) copy-start(f32[256]{0:T(256)S(1)} %get-tuple-element.294) | copy-start | bytes 3076
  386.5 43.0 %copy-start.104 = (f32[256]{0:T(256)}, f32[256]{0:T(256)S(1)}, u32[]{:S(2)}) copy-start(f32[256]{0:T(256)S(1)} %get-tuple-element.234) | copy-start | bytes 3076
  386.5 22.4 %slice-start.4 = ((s8[4718592]{0:T(1024)(128)(4,1)}), s8[4194304]{0:T(1024)(128)(4,1)S(1)}, s32[]{:S(2)}) async-start(s8[4718592]{0:T(1024)(128)(4,1)} %bitcast.494), calls=%async_computation.28 | async-start | bytes 8388608
  412.4 13.0 %all-to-all-start.9 = ((bf16[4,128,768]{1,2,0:T(8,128)(2,1)}), bf16[4,128,768]{1,2,0:T(8,128)(2,1)}, u32[]{:S(2)}, u32[]{:S(2)}) async-start(bf16[4,128,768]{1,2,0:T(8,128)(2,1)} %fusion.130), calls=%async_computation.9 | async-start | bytes 1572864 | tf_op jit(solution)/shard_map/all_to_all | solution.py:468
  432.2 13.0 %slice-start.2 = ((s8[4718592]{0:T(1024)(128)(4,1)}), s8[4194304]{0:T(1024)(128)(4,1)S(1)}, s32[]{:S(2)}) async-start(s8[4718592]{0:T(1024)(128)(4,1)} %bitcast.488), calls=%async_computation.26 | async-start | bytes 8388608
  433.6 13.5 %copy-start.27 = (f32[256,768]{1,0:T(8,128)}, f32[256,768]{1,0:T(8,128)S(1)}, u32[]{:S(2)}) copy-start(f32[256,768]{1,0:T(8,128)S(1)} %convert_add_fusion.3) | copy-start | bytes 2359300
  448.4 11.3 %collective-permute-start.6 = (bf16[256,768]{1,0:T(8,128)(2,1)}, bf16[256,768]{1,0:T(8,128)(2,1)}, u32[]{:S(2)}, u32[]{:S(2)}) collective-permute-start(bf16[256,768]{1,0:T(8,128)(2,1)} %get-tuple-element.226), channel_id=1, source_target_pairs={{16,0},{17,1},{18,2},{19,3},{20,4},{21,5},{22,6},{23,7},{24,8},{25... | collective-permute-start | bytes 1179656 | tf_op jit(solution)/shard_map/ppermute | solution.py:55
  459.7 42.3 %collective-permute-start.7 = (bf16[1,768,3072]{2,1,0:T(8,128)(2,1)}, bf16[1,768,3072]{2,1,0:T(8,128)(2,1)}, u32[]{:S(2)}, u32[]{:S(2)}) collective-permute-start(bf16[1,768,3072]{2,1,0:T(8,128)(2,1)} %get-tuple-element.123), channel_id=1, source_target_pairs={{16,0},{17,1},{18,2},{19,3},{20,4},{21,5},{22,6},{23,7},{24,8},{25... | collective-permute-start | bytes 14155784 | tf_op jit(solution)/shard_map/ppermute | solution.py:528
  462.5 91.8 %copy-start.73 = (f32[256]{0:T(256)}, f32[256]{0:T(256)S(1)}, u32[]{:S(2)}) copy-start(f32[256]{0:T(256)S(1)} %get-tuple-element.227) | copy-start | bytes 3076
  464.6 42.3 %all-to-all-start.11 = ((bf16[4,128,768]{2,1,0:T(8,128)(2,1)}), bf16[4,128,768]{2,1,0:T(8,128)(2,1)}, u32[]{:S(2)}, u32[]{:S(2)}) async-start(bf16[4,128,768]{2,1,0:T(8,128)(2,1)} %bitcast.502), calls=%async_computation.11 | async-start | bytes 1572864 | tf_op jit(solution)/shard_map/all_to_all | solution.py:448
  468.8 124.9 %reduce-scatter.4.cloned.1.call-start = ((), (), s32[]{:S(2)}) async-start(), calls=%async_computation.20 | async-start | bytes 5898240 | tf_op jit(solution)/shard_map/reduce_scatter | solution.py:314
  539.7 43.4 %collective-permute-start.8 = (bf16[1,768,3072]{2,1,0:T(8,128)(2,1)}, bf16[1,768,3072]{2,1,0:T(8,128)(2,1)}, u32[]{:S(2)}, u32[]{:S(2)}) collective-permute-start(bf16[1,768,3072]{2,1,0:T(8,128)(2,1)} %get-tuple-element.131), channel_id=1, source_target_pairs={{0,16},{1,17},{2,18},{3,19},{4,20},{5,21},{6,22},{7,23},{8,24},{9,... | collective-permute-start | bytes 14155784 | tf_op jit(solution)/shard_map/ppermute | solution.py:463
  550.1 12.3 %all-to-all-start.12 = ((bf16[4,128,768]{1,2,0:T(8,128)(2,1)}), bf16[4,128,768]{1,2,0:T(8,128)(2,1)}, u32[]{:S(2)}, u32[]{:S(2)}) async-start(bf16[4,128,768]{1,2,0:T(8,128)(2,1)} %fusion.125), calls=%async_computation.12 | async-start | bytes 1572864 | tf_op jit(solution)/shard_map/all_to_all | solution.py:468
  554.3 143.7 %reduce-scatter.6.cloned.1.call-start = ((), (), s32[]{:S(2)}) async-start(), calls=%async_computation.21 | async-start | bytes 5898240 | tf_op jit(solution)/shard_map/reduce_scatter | solution.py:314
  554.4 14.5 %copy-start.88 = (f32[256]{0:T(256)}, f32[256]{0:T(256)S(1)}, u32[]{:S(2)}) copy-start(f32[256]{0:T(256)S(1)} %mul.655) | copy-start | bytes 3076
  593.8 135.8 %reduce-scatter.8.cloned.1.call-start = ((), (), s32[]{:S(2)}) async-start(), calls=%async_computation.22 | async-start | bytes 1720320 | tf_op jit(solution)/shard_map/reduce_scatter | solution.py:561
  601.9 11.6 %copy-start.13 = (bf16[256,768]{1,0:T(8,128)(2,1)S(1)}, bf16[256,768]{1,0:T(8,128)(2,1)}, u32[]{:S(2)}) copy-start(bf16[256,768]{1,0:T(8,128)(2,1)} %copy-done.12) | copy-start | bytes 1179652
  603.2 10.9 %copy-start.17 = (bf16[256,768]{1,0:T(8,128)(2,1)S(1)}, bf16[256,768]{1,0:T(8,128)(2,1)}, u32[]{:S(2)}) copy-start(bf16[256,768]{1,0:T(8,128)(2,1)} %copy-done.16) | copy-start | bytes 1179652
  603.2 10.9 %copy-start.28 = (f32[256,768]{1,0:T(8,128)S(1)}, f32[256,768]{1,0:T(8,128)}, u32[]{:S(2)}) copy-start(f32[256,768]{1,0:T(8,128)} %copy-done.27) | copy-start | bytes 2359300
  701.2 2.8 collective-permute-start.9
  731.7 18.6 %all-to-all-start.14 = ((bf16[4,48,3072]{2,1,0:T(8,128)(2,1)}), bf16[4,48,3072]{2,1,0:T(8,128)(2,1)S(1)}, u32[]{:S(2)}, u32[]{:S(2)}) async-start(bf16[4,48,3072]{2,1,0:T(8,128)(2,1)} %broadcast_in_dim.82), calls=%async_computation.17 | async-start | bytes 2359296 | tf_op jit(solution)/shard_map/all_to_all | solution.py:256
  (95 other events, 429.2 us)
Sparse Core Ops, SparseCore 0:
  10.2 33.1 all-gather.9
  46.4 88.7 all-gather.5
  139.1 90.6 all-gather.7
  507.1 86.5 reduce-scatter.3
  595.9 85.7 reduce-scatter.5
  698.2 31.3 reduce-scatter.7
